TPU v7x, 256 devices: a whole 4x4x8 slice. The times are simulated.
256 devices in a mesh: ctx: 64 (over z, y, core), head: 4 (over x).
Axes of the slice: x: 4, y: 4, z: 8, core: 2. Of those that a mesh axis runs over, the one named last changes fastest.
Arguments:
- queries: bfloat16 [24576, 64, 128], P('ctx', 'head'), may hold values from -12 to 12
- keys: bfloat16 [8, 262144, 128], P('head', 'ctx'), may hold values from -8 to 8
- values: bfloat16 [8, 262144, 128], P('head', 'ctx'), may hold values from -6 to 6
- sel_blocks: int32 [384, 8, 16], P('ctx', 'head'), may hold values from 0 to 4095, as said below
- sel_counts: int32 [384, 8], P('ctx', 'head'), may hold values from 8 to 16, as said below
Outputs:
- attended: bfloat16 [24576, 8192], P(('ctx', 'head'))
Inputs may be any that keep to these rules, and one draw needn't show every extreme that they name: For each (b, g) the first sel_counts[b, g] entries of sel_blocks[b, g] are distinct; later entries are arbitrary block numbers that are not used. The rows of one device are the (b, g) with equal b // 6 and equal g // 2: of the used entries of one device's rows, at most 6 name blocks j with equal j // 64, and on every device some value of j // 64 gets exactly 6. `sel_counts`: among the rows of each device at least one (b, g) has the count 16.
All inputs are finite; a program needn't handle non-finite values.
Results may differ from a plain program's by a relative error of at most 0.0049.
Values may be sent and summed in bfloat16 or wider, within the bound.
A program may use at most 128 MiB of HBM per device.

v0:
```python
from functools import partial

import jax
import jax.numpy as jnp
from jax import lax
from jax.sharding import PartitionSpec as P

BLK = 64


def weighting(query_rows, key_rows, kept_keys, scaling):
    scores = jnp.dot(query_rows, key_rows.T, preferred_element_type=jnp.float32) * scaling
    scores = jnp.where(kept_keys[None, :], scores, -jnp.inf)
    largest = jnp.max(scores, axis=1, keepdims=True)
    exponent = jnp.exp(scores - largest)
    return (exponent / jnp.sum(exponent, axis=1, keepdims=True)).astype(jnp.bfloat16)


def attend(query_rows, key_rows, value_rows, kept_keys, scaling):
    weights = weighting(query_rows, key_rows, kept_keys, scaling)
    return jnp.dot(weights, value_rows, preferred_element_type=jnp.float32).astype(jnp.bfloat16)


def live_slots(blocks, counts):
    chosen_count = blocks.shape[2]
    slot_ids = jnp.arange(blocks.shape[0] * blocks.shape[1] * chosen_count)
    return (slot_ids, slot_ids % chosen_count < jnp.repeat(counts.reshape(-1), chosen_count))


def request_row(blocks, counts, target, kb_dev, capacity):
    chosen_count = blocks.shape[2]
    g_dev = blocks.shape[1]
    flat_blocks = blocks.reshape(-1)
    slot_ids, live_slot = live_slots(blocks, counts)
    holder = flat_blocks // kb_dev
    own_slot = (live_slot & (holder == target)).astype(jnp.int32)
    standing = jnp.cumsum(own_slot) - own_slot
    tile_id = slot_ids // chosen_count % g_dev * kb_dev + flat_blocks % kb_dev
    matches = (own_slot[:, None] == 1) & (standing[:, None] == jnp.arange(capacity)[None, :])
    return jnp.sum(jnp.where(matches, tile_id[:, None] + 1, 0), axis=0) - 1


def owner_rank(holder, live_slot, n_ctx):
    onehot = ((holder[:, None] == jnp.arange(n_ctx)[None, :]) & live_slot[:, None]).astype(
        jnp.int32
    )
    before = jnp.cumsum(onehot, axis=0) - onehot
    return jnp.sum(before * onehot, axis=1)


def per_device(queries, keys, values, sel_blocks, sel_counts):
    n_ctx = lax.axis_size("ctx")
    qb_dev, g_dev, chosen_count = sel_blocks.shape
    block_len = BLK
    hd_width = keys.shape[2]
    kb_dev = keys.shape[1] // block_len
    per_group = queries.shape[1] // g_dev
    capacity = max(2, 2 * qb_dev * g_dev * chosen_count // n_ctx)
    item_count = qb_dev * g_dev
    scaling = hd_width ** (-0.5)
    builder = partial(request_row, sel_blocks, sel_counts, kb_dev=kb_dev, capacity=capacity)
    slot_table = jax.vmap(builder)(jnp.arange(n_ctx, dtype=jnp.int32))
    incoming = lax.all_to_all(slot_table, "ctx", split_axis=0, concat_axis=0, tiled=True)
    tile_ids = jnp.maximum(incoming, 0)
    key_table = keys.reshape(g_dev * kb_dev, block_len, hd_width)
    value_table = values.reshape(g_dev * kb_dev, block_len, hd_width)
    key_out = jnp.take(key_table, tile_ids, axis=0)
    value_out = jnp.take(value_table, tile_ids, axis=0)
    flat_blocks = sel_blocks.reshape(-1)
    slot_ids, live_slot = live_slots(sel_blocks, sel_counts)
    holder = flat_blocks // kb_dev
    standing = owner_rank(holder, live_slot, n_ctx)
    where_from = jnp.where(live_slot, holder * capacity + standing, 0)
    query_items = queries.reshape(qb_dev, block_len, g_dev, per_group, hd_width).transpose(
        0, 2, 1, 3, 4
    )
    query_items = query_items.reshape(item_count, block_len * per_group, hd_width)
    kept_keys = (
        jnp.arange(chosen_count * block_len)[None, :] // block_len
        < sel_counts.reshape(item_count)[:, None]
    )

    def select_tiles(received):
        flat_tiles = received.reshape(n_ctx * capacity, block_len, hd_width)
        return jnp.take(flat_tiles, where_from, axis=0).reshape(
            item_count, chosen_count * block_len, hd_width
        )

    key_in, value_in = (
        lax.all_to_all(key_out, "ctx", split_axis=0, concat_axis=0, tiled=True),
        lax.all_to_all(value_out, "ctx", split_axis=0, concat_axis=0, tiled=True),
    )

    def attend_item(packed):
        return attend(packed[0], packed[1], packed[2], packed[3], scaling)

    attended = lax.map(
        attend_item, (query_items, select_tiles(key_in), select_tiles(value_in), kept_keys)
    )
    merged = attended.reshape(qb_dev, g_dev, block_len, per_group, hd_width).transpose(
        0, 2, 1, 3, 4
    )
    merged = merged.reshape(qb_dev * block_len, g_dev * per_group * hd_width)
    return lax.all_to_all(merged, "head", split_axis=0, concat_axis=1, tiled=True)


def solution(mesh):
    placed = (
        P("ctx", "head", None),
        P("head", "ctx", None),
        P("head", "ctx", None),
        P("ctx", "head", None),
        P("ctx", "head"),
    )
    return jax.shard_map(
        per_device, mesh=mesh, in_specs=placed, out_specs=P(("ctx", "head"), None), check_vma=False
    )
```

profile of v0, /device:TPU:1, one launch (start us, length us, event | category | flops | bytes accessed | tf_op | source)
XLA Modules:
  0.0 433.6 jit_solution(12646187432449761329)
XLA Ops:
  0.0 0.9 copy.27
  1.2 0.8 reshape.252
  2.0 0.6 reduce-window.12
  3.3 22.3 %all_to_all.35 = s32[64,1,6]{2,1,0:T(1,128)S(1)} all-to-all(s32[64,1,6]{2,1,0:T(1,128)S(1)} %copy.31), channel_id=1, replica_groups=mesh['ctx'=64,'head'=4] {'ctx'}, dimensions={0} | all-to-all | bytes 3072 | tf_op jit(solution)/shard_map/all_to_all | solution.py:63
  25.8 13.3 %gather_fusion = bf16[384,64,128]{2,1,0:T(8,128)(2,1)} fusion(bf16[128,64,128]{2,1,0:T(8,128)(2,1)S(1)} %bitcast.63, s32[1024]{0:T(1024)S(1)} %pad_clamp_fusion.1), kind=kCustom, calls=%fused_computation.clone | custom fusion | bytes 12584448 | tf_op jit(solution)/shard_map/jit(_take)/gather | solution.py:67
  39.1 5.6 %gather_fusion.2 = bf16[384,64,128]{2,1,0:T(8,128)(2,1)} fusion(bf16[128,64,128]{2,1,0:T(8,128)(2,1)} %bitcast.66, s32[1024]{0:T(1024)S(1)} %pad_clamp_fusion.1), kind=kCustom, calls=%fused_computation.2.clone | custom fusion | bytes 12584448 | tf_op jit(solution)/shard_map/jit(_take)/gather | solution.py:68
  44.7 8.3 %broadcast_select_fusion = (bf16[64,6,64,128]{3,2,1,0:T(8,128)(2,1)}, bf16[64,6,64,128]{3,2,1,0:T(8,128)(2,1)S(1)}) fusion(bf16[64,6,64,128]{3,2,1,0:T(8,128)(2,1)} %bitcast.65, pred[64,6]{1,0:T(8,128)(4,1)S(1)} %compare_and_fusion, bf16[64,6,64,128]{3,2,1,0:T(8,128)(2,1)} %bitcast.64), kind=kLoop, calls=%fused_computation.25 | loop fusion | flops 6291456 | bytes 25166208 | tf_op jit(solution)/shard_map/jit(_take)/select_n | solution.py:68
  53.1 144.2 %all_to_all.36 = bf16[64,6,64,128]{3,2,1,0:T(8,128)(2,1)} all-to-all(bf16[64,6,64,128]{3,2,1,0:T(8,128)(2,1)S(1)} %get-tuple-element.59), channel_id=1, replica_groups=mesh['ctx'=64,'head'=4] {'ctx'}, dimensions={0} | all-to-all | bytes 12582912 | tf_op jit(solution)/shard_map/all_to_all | solution.py:90
  197.3 7.4 %all-to-all-start.2 = ((bf16[64,6,64,128]{3,2,1,0:T(8,128)(2,1)}), bf16[64,6,64,128]{3,2,1,0:T(8,128)(2,1)}, u32[]{:S(2)}, u32[]{:S(2)}) async-start(bf16[64,6,64,128]{3,2,1,0:T(8,128)(2,1)} %get-tuple-element.58), calls=%async_computation.2 | async-start | bytes 12582912 | tf_op jit(solution)/shard_map/all_to_all | solution.py:91
  204.7 1.5 copy.28
  206.4 5.5 %gather_fusion.1 = bf16[192,64,128]{2,1,0:T(8,128)(2,1)} fusion(bf16[384,64,128]{2,1,0:T(8,128)(2,1)} %bitcast.67, s32[1024]{0:T(1024)S(1)} %pad_clamp_fusion), kind=kCustom, calls=%fused_computation.1.clone | custom fusion | bytes 6292224 | tf_op jit(solution)/shard_map/jit(_take)/gather | solution.py:85
  211.9 131.6 %all-to-all-done.2 = bf16[64,6,64,128]{3,2,1,0:T(8,128)(2,1)} async-done(((bf16[64,6,64,128]{3,2,1,0:T(8,128)(2,1)}), bf16[64,6,64,128]{3,2,1,0:T(8,128)(2,1)}, u32[]{:S(2)}, u32[]{:S(2)}) %all-to-all-start.2) | async-done | bytes 6291488 | tf_op jit(solution)/shard_map/all_to_all | solution.py:91
  343.5 5.5 %gather_fusion.3 = bf16[192,64,128]{2,1,0:T(8,128)(2,1)} fusion(bf16[384,64,128]{2,1,0:T(8,128)(2,1)} %bitcast.16, s32[1024]{0:T(1024)S(1)} %pad_clamp_fusion), kind=kCustom, calls=%fused_computation.3.clone | custom fusion | bytes 6292224 | tf_op jit(solution)/shard_map/jit(_take)/gather | solution.py:85
  349.0 5.0 %broadcast_select_fusion.2 = (bf16[192,64,128]{2,1,0:T(8,128)(2,1)}, bf16[192,64,128]{2,1,0:T(8,128)(2,1)}) fusion(bf16[192,64,128]{2,1,0:T(8,128)(2,1)} %gather_fusion.3, pred[192]{0:T(512)(128)(4,1)S(1)} %get-tuple-element.52, bf16[192,64,128]{2,1,0:T(8,128)(2,1)} %gather_fusion.1), kind=kLoop, calls=%fused_computation.27 | loop fusion | flops 3145728 | bytes 12583104 | tf_op jit(solution)/shard_map/jit(_take)/select_n | solution.py:85
  354.1 52.9 %while.10 = (s32[]{:T(128)}, bf16[12,512,128]{2,1,0:T(8,128)(2,1)}, pred[12,1024]{1,0:T(8,128)(4,1)S(1)}, bf16[12,512,128]{2,1,0:T(8,128)(2,1)}, bf16[12,1024,12...) while((s32[]{:T(128)}, bf16[12,512,128]{2,1,0:T(8,128)(2,1)}, ...), condition=%wide.region_7.10_spmd, body=%wide.region_4.9_spmd.sunk | while | flops 274791424 | bytes 7095377 | solution.py:97
  354.1 1.5 fusion.38
  356.2 2.3 fusion.40
  358.5 1.5 fusion.38
  360.0 0.6 fusion.39
  360.6 2.3 fusion.40
  362.9 1.5 fusion.38
  365.0 2.3 fusion.40
  367.3 1.5 fusion.38
  368.8 0.6 fusion.39
  369.4 2.3 fusion.40
  371.7 1.5 fusion.38
  373.2 0.6 fusion.39
  373.8 2.3 fusion.40
  376.1 1.5 fusion.38
  377.6 0.6 fusion.39
  378.2 2.3 fusion.40
  380.5 1.5 fusion.38
  382.1 0.6 fusion.39
  382.6 2.3 fusion.40
  384.9 1.5 fusion.38
  387.0 2.3 fusion.40
  389.3 1.5 fusion.38
  391.4 2.3 fusion.40
  393.7 1.5 fusion.38
  395.8 2.3 fusion.40
  398.1 1.5 fusion.38
  400.2 2.3 fusion.40
  402.5 1.5 fusion.38
  404.6 2.3 fusion.40
  406.9 1.7 copy.42
  408.6 2.1 all_to_all.27
  410.6 21.7 %all_to_all.37 = bf16[4,96,2048]{2,1,0:T(8,128)(2,1)S(1)} all-to-all(bf16[4,96,2048]{2,1,0:T(8,128)(2,1)} %all_to_all.27), channel_id=1, replica_groups=mesh['ctx'=64,'head'=4] {'head'}, dimensions={0} | all-to-all | bytes 3145728 | tf_op jit(solution)/shard_map/all_to_all | solution.py:104
  432.3 1.2 copy.36
  (51 shorter events, 5.6 us)
Async XLA Ops:
  0.0 25.8 %copy-start = (bf16[2,4096,128]{2,1,0:T(8,128)(2,1)S(1)}, bf16[2,4096,128]{2,1,0:T(8,128)(2,1)}, u32[]{:S(2)}) copy-start(bf16[2,4096,128]{2,1,0:T(8,128)(2,1)} %param.12) | copy-start | bytes 6291460
  197.3 7.4 %copy-start.2 = (bf16[384,16,128]{2,1,0:T(8,128)(2,1)S(1)}, bf16[384,16,128]{2,1,0:T(8,128)(2,1)}, u32[]{:S(2)}) copy-start(bf16[384,16,128]{2,1,0:T(8,128)(2,1)} %param.11) | copy-start | bytes 4718596
  197.3 146.3 %all-to-all-start.2 = ((bf16[64,6,64,128]{3,2,1,0:T(8,128)(2,1)}), bf16[64,6,64,128]{3,2,1,0:T(8,128)(2,1)}, u32[]{:S(2)}, u32[]{:S(2)}) async-start(bf16[64,6,64,128]{3,2,1,0:T(8,128)(2,1)} %get-tuple-element.58), calls=%async_computation.2 | async-start | bytes 12582912 | tf_op jit(solution)/shard_map/all_to_all | solution.py:91
  410.6 22.9 %copy-start.1 = (bf16[2,4096,128]{2,1,0:T(8,128)(2,1)S(1)}, bf16[2,4096,128]{2,1,0:T(8,128)(2,1)}, u32[]{:S(2)}) copy-start(bf16[2,4096,128]{2,1,0:T(8,128)(2,1)} %param.12) | copy-start | bytes 6291460
where the time goes:
time: 439 us; the launch traced here: 434 us
  blocking collectives  188 us (43%)
  waiting for transfers between devices  132 us (30%)
  matrix products  45.6 us (10%)
  local copies, waits for them, and re-layouts  39.1 us (9%)
  other arithmetic  21.4 us (5%)
  starting transfers between devices  7.43 us (2%)
    all_to_all x1, blocking collectives, per_device(): lax.all_to_all(key_out, 'ctx', split_axis=0, concat_axis=0, tiled=True)  144 us
    all_to_all x1, waiting for transfers between devices, per_device(): lax.all_to_all(value_out, 'ctx', split_axis=0, concat_axis=0, tiled=True)  132 us
    dot_general x12, matrix products, attend(): jnp.dot(weights, value_rows, preferred_element_type=jnp.float32)  27.1 us
    all_to_all x1, blocking collectives, per_device(): lax.all_to_all(slot_table, 'ctx', split_axis=0, concat_axis=0, tiled=True)  22.3 us
    all_to_all x1, blocking collectives, per_device(): lax.all_to_all(merged, 'head', split_axis=0, concat_axis=1, tiled=True)  21.7 us
    dot_general x12, matrix products, weighting(): jnp.dot(query_rows, key_rows.T, preferred_element_type=jnp.float32)  18.5 us
    gather x1, local copies, waits for them, and re-layouts, per_device(): key_out = jnp.take(key_table, tile_ids, axis=0)  13.3 us
    gather x2, local copies, waits for them, and re-layouts, select_tiles(): jnp.take(flat_tiles, where_from, axis=0)  11 us
  transfers between devices with their start and end apart: 1, of which 1 were waited for; matrix products, arithmetic and copies ran while one was open for 2% of the time, Pallas kernels for 0%

commit v1 on v0

v1 whole, which is shorter than its diff:
```python
import jax
import jax.numpy as jnp
import numpy as np
from jax import lax
from jax.experimental import pallas as pl
from jax.experimental.pallas import tpu as pltpu
from jax.sharding import PartitionSpec as P

BLK = 64
HD = 128
SEL = 16
ITEMS = 12
NZ = 8
NW = 8
STEPS = 4
USUAL = (108, 84, 56, 24)
FULL = (168, 120, 72, 24)
MESH = pl.DeviceIdType.MESH


def at_ctx(index):
    return {"ctx": index}


def requests_kernel(mine, k_own, table, k_twin, local_sem, send_sem, recv_sem):
    me = lax.axis_index("ctx")
    z, w = me // NW, me % NW
    barrier = pltpu.get_barrier_semaphore()
    for r in range(1, 8):
        pl.semaphore_signal(barrier, inc=1, device_id=at_ctx(z * NW + (w + r) % NW), device_id_type=MESH)
        pl.semaphore_signal(barrier, inc=1, device_id=at_ctx((z + r) % NZ * NW + w), device_id_type=MESH)
    pl.semaphore_wait(barrier, 14)

    own = pltpu.make_async_copy(mine.at[pl.ds(w, 1)], table.at[pl.ds(w, 1)], local_sem)
    own.start()
    inside = []
    for r in range(1, NW):
        ow = (w + r) % NW
        copy = pltpu.make_async_remote_copy(
            src_ref=mine.at[pl.ds(ow, 1)], dst_ref=table.at[pl.ds(w, 1)],
            send_sem=send_sem.at[r], recv_sem=recv_sem.at[r],
            device_id=at_ctx(z * NW + ow), device_id_type=MESH,
        )
        copy.start()
        inside.append(copy)
    twin = me + 1 - 2 * (me % 2)
    keys_over = pltpu.make_async_remote_copy(
        src_ref=k_own, dst_ref=k_twin, send_sem=send_sem.at[0], recv_sem=recv_sem.at[0],
        device_id=at_ctx(twin), device_id_type=MESH,
    )
    keys_over.start()
    own.wait()
    for copy in inside:
        copy.wait()
    along = []
    for r in range(1, NZ):
        copy = pltpu.make_async_remote_copy(
            src_ref=table.at[pl.ds(0, NW)], dst_ref=table.at[pl.ds((NZ - r) * NW, NW)],
            send_sem=send_sem.at[NW + r], recv_sem=recv_sem.at[NW + r],
            device_id=at_ctx((z + r) % NZ * NW + w), device_id_type=MESH,
        )
        copy.start()
        along.append(copy)
    for copy in along:
        copy.wait()
    keys_over.wait()


def exchange_requests(mine, k_own):
    vmem, anywhere = pl.BlockSpec(memory_space=pltpu.VMEM), pl.BlockSpec(memory_space=pl.ANY)
    return pl.pallas_call(
        requests_kernel,
        out_shape=(
            jax.ShapeDtypeStruct((NZ * NW, 1, 128), jnp.int32),
            jax.ShapeDtypeStruct(k_own.shape, k_own.dtype),
        ),
        in_specs=[vmem, anywhere],
        out_specs=(vmem, anywhere),
        scratch_shapes=[
            pltpu.SemaphoreType.DMA,
            pltpu.SemaphoreType.DMA((16,)),
            pltpu.SemaphoreType.DMA((16,)),
        ],
        compiler_params=pltpu.CompilerParams(collective_id=0, has_side_effects=True),
        name="requests",
    )(mine, k_own)


def tiles_kernel(caps, arrays, fetch, src, post, over, *refs):
    cuts = (0, *caps[::-1])
    refs = list(refs)
    take = lambda n: [refs.pop(0) for _ in range(n)]
    owns = take(arrays)
    twins = [None if f else refs.pop(0) for f in fetch]
    outs, over_out = take(arrays), refs.pop(0)
    tab, lists, stage = take(arrays), take(arrays), take(arrays)
    hops = [take(STEPS) for _ in range(arrays)]
    overs, tab_sem, twin_send, z_send, z_recv, y_send, y_recv, y_local, over_send, over_recv = refs
    me = lax.axis_index("ctx")
    z, w = me // NW, me % NW
    core = me % 2
    twin_at = me + 1 - 2 * core
    towards = (((z + 1) % NZ) * NW + w, ((z + NZ - 1) % NZ) * NW + w)

    barrier = pltpu.get_barrier_semaphore()
    for other in towards:
        pl.semaphore_signal(barrier, inc=1, device_id=at_ctx(other), device_id_type=MESH)
    for r in range(1, NW):
        pl.semaphore_signal(barrier, inc=1, device_id=at_ctx(z * NW + (w + r) % NW), device_id_type=MESH)
    pl.semaphore_wait(barrier, NW + 1)

    loads = []
    for a in range(arrays):
        mine = tab[a].at[pl.ds(core * 128, 128)]
        pair = [pltpu.make_async_copy(owns[a], mine, tab_sem.at[a, 0])]
        if fetch[a]:
            pair.append(
                pltpu.make_async_remote_copy(
                    src_ref=owns[a], dst_ref=mine, send_sem=twin_send.at[a], recv_sem=tab_sem.at[a, 1],
                    device_id=at_ctx(twin_at), device_id_type=MESH,
                )
            )
        else:
            pair.append(
                pltpu.make_async_copy(twins[a], tab[a].at[pl.ds((1 - core) * 128, 128)], tab_sem.at[a, 1])
            )
        for copy in pair:
            copy.start()
        loads.append(pair)
    told = []
    for r in range(1, NW):
        copy = pltpu.make_async_remote_copy(
            src_ref=over, dst_ref=overs.at[r], send_sem=over_send.at[r], recv_sem=over_recv.at[r],
            device_id=at_ctx(z * NW + (w + r) % NW), device_id_type=MESH,
        )
        copy.start()
        told.append(copy)

    def hop(a, d, step, piece):
        lo, hi = cuts[piece], cuts[piece + 1]
        source = lists[a] if step == 1 else hops[a][step - 2]
        number = (0, 4, 7, 9)[step - 1] + piece
        return pltpu.make_async_remote_copy(
            src_ref=source.at[d, pl.ds(lo, hi - lo)],
            dst_ref=hops[a][step - 1].at[d, pl.ds(lo, hi - lo)],
            send_sem=z_send.at[a, d, number],
            recv_sem=z_recv.at[a, d, number],
            device_id=at_ctx(towards[d]),
            device_id_type=MESH,
        )

    def pack(a, piece):
        for d in range(2):
            def one(i, carry):
                lists[a][d, i] = tab[a][src[d * caps[0] + i]]
                return carry

            lax.fori_loop(cuts[piece], cuts[piece + 1], one, 0)

    def deliver(a, k):
        base = k * NW * 6
        if k == 4:
            def both(i, carry):
                at = base + i
                for d in range(2):
                    for s in range(6):
                        stage[a][base + (2 * i + d) * 6 + s] = hops[a][3][d, post[base + (2 * i + d) * 6 + s]]
                return carry

            lax.fori_loop(0, NW // 2, both, 0)
        else:
            def one(i, carry):
                index = post[base + i]
                if k == 0:
                    tile = tab[a][index]
                elif k < 4:
                    tile = hops[a][k - 1][0, index]
                else:
                    tile = hops[a][7 - k][1, index]
                stage[a][base + i] = tile
                return carry

            lax.fori_loop(0, NW * 6, one, 0)

        def send(r, carry):
            ow = (w + r) % NW
            pltpu.make_async_remote_copy(
                src_ref=stage[a].at[pl.ds(base + ow * 6, 6)],
                dst_ref=outs[a].at[pl.ds(base + w * 6, 6)],
                send_sem=y_send.at[a],
                recv_sem=y_recv.at[a],
                device_id=at_ctx(z * NW + ow),
                device_id_type=MESH,
            ).start()
            return carry

        lax.fori_loop(1, NW, send, 0)
        pltpu.make_async_copy(
            stage[a].at[pl.ds(base + w * 6, 6)], outs[a].at[pl.ds(base + w * 6, 6)], y_local.at[a]
        ).start()

    def arrive_and_pass(a, step):
        for piece in range(5 - step):
            for d in range(2):
                hop(a, d, step, piece).wait_recv()
                if piece < 4 - step:
                    hop(a, d, step + 1, piece).start()

    def start_first(a):
        for piece in range(STEPS):
            for d in range(2):
                hop(a, d, 1, piece).start()

    for copy in loads[0]:
        copy.wait()
    for piece in range(STEPS):
        pack(0, piece)
        for d in range(2):
            hop(0, d, 1, piece).start()
    if arrays == 2:
        for copy in loads[1]:
            copy.wait()
        for piece in range(STEPS):
            pack(1, piece)
    deliver(0, 0)
    arrive_and_pass(0, 1)
    if arrays == 2:
        start_first(1)
        deliver(1, 0)
    for a in range(arrays):
        if a:
            arrive_and_pass(a, 1)
        for step in range(1, STEPS):
            deliver(a, step)
            deliver(a, NZ - step)
            arrive_and_pass(a, step + 1)
        deliver(a, STEPS)
    for a in range(arrays):
        for d in range(2):
            for step in range(1, STEPS + 1):
                for piece in range(STEPS + 1 - step):
                    hop(a, d, step, piece).wait_send()
    most = over[...]
    for r, copy in enumerate(told):
        copy.wait()
        most = jnp.maximum(most, overs[r + 1])
    over_out[...] = most
    remote, local = NZ * (NW - 1) * 6, NZ * 6
    for a in range(arrays):
        pltpu.make_async_copy(stage[a].at[pl.ds(0, remote)], stage[a].at[pl.ds(0, remote)], y_send.at[a]).wait()
        pltpu.make_async_copy(outs[a].at[pl.ds(0, remote)], outs[a].at[pl.ds(0, remote)], y_recv.at[a]).wait()
        pltpu.make_async_copy(outs[a].at[pl.ds(0, local)], outs[a].at[pl.ds(0, local)], y_local.at[a]).wait()


def exchange_tiles(number, caps, src, post, over, owns, twins):
    n = len(owns)
    fetch = tuple(t is None for t in twins)
    given = [t for t in twins if t is not None]
    tiles = jax.ShapeDtypeStruct((NZ * NW * 6, BLK, HD), owns[0].dtype)
    vmem = lambda *shape: pltpu.VMEM((*shape, BLK, HD), jnp.bfloat16)
    smem, whole = pl.BlockSpec(memory_space=pltpu.SMEM), pl.BlockSpec(memory_space=pltpu.VMEM)
    anywhere = pl.BlockSpec(memory_space=pl.ANY)
    dma = pltpu.SemaphoreType.DMA
    return pl.pallas_call(
        lambda *refs: tiles_kernel(caps, n, fetch, *refs),
        out_shape=(*[tiles] * n, jax.ShapeDtypeStruct((1, 128), jnp.int32)),
        in_specs=[smem, smem, whole, *[anywhere] * (n + len(given))],
        out_specs=(*[anywhere] * n, whole),
        scratch_shapes=[
            *[vmem(256)] * n,
            *[vmem(2, caps[0])] * n,
            *[vmem(NZ * NW * 6)] * n,
            *[vmem(2, c) for c in caps] * n,
            pltpu.VMEM((NW, 1, 128), jnp.int32),
            dma((n, 2)), dma((n,)), dma((n, 2, 10)), dma((n, 2, 10)),
            dma((n,)), dma((n,)), dma((n,)), dma((NW,)), dma((NW,)),
        ],
        compiler_params=pltpu.CompilerParams(
            collective_id=number, has_side_effects=True, vmem_limit_bytes=60 * 2**20
        ),
        name="tiles",
    )(src, post, over, *owns, *given)


def attend_kernel(where, counts, over, q, k, v, out, over_out, merged, qf, kc, vc, overs, send_sem, recv_sem, own_sem, over_send, over_recv):
    me = lax.axis_index("head")
    barrier = pltpu.get_barrier_semaphore()
    for r in range(1, 4):
        pl.semaphore_signal(barrier, inc=1, device_id={"head": (me + r) % 4}, device_id_type=MESH)
    pl.semaphore_wait(barrier, 3)
    told = []
    for r in range(1, 4):
        copy = pltpu.make_async_remote_copy(
            src_ref=over, dst_ref=overs.at[r], send_sem=over_send.at[r], recv_sem=over_recv.at[r],
            device_id={"head": (me + r) % 4}, device_id_type=MESH,
        )
        copy.start()
        told.append(copy)
    keys = SEL * BLK
    factor = float(HD ** -0.5 * np.log2(np.e))
    vc[:, HD:] = jnp.ones((keys, HD), jnp.bfloat16)
    first = ((me + 1) * 3 // 2) % 6

    def one_block(i, carry):
        b = (first + i) % 6
        qf[...] = q[pl.ds(b * BLK, BLK)].astype(jnp.float32).reshape(BLK * 16, HD)
        for g in range(2):
            item = b * 2 + g

            def gather(s, c):
                at = where[item * SEL + s]
                kc[pl.ds(s * BLK, BLK)] = k[at]
                vc[pl.ds(s * BLK, BLK), 0:HD] = v[at]
                return c

            lax.fori_loop(0, SEL, gather, 0)
            rows = jnp.concatenate(
                [qf[pl.ds(g * 8 + h, BLK, stride=16)].astype(jnp.bfloat16) for h in range(8)], axis=0
            )
            s = lax.dot_general(rows, kc[...], (((1,), (1,)), ((), ())), preferred_element_type=jnp.float32)
            kept = lax.broadcasted_iota(jnp.int32, (1, keys), 1) < counts[item] * BLK
            s = jnp.where(kept, s, -jnp.inf)
            top = jnp.max(s, axis=1, keepdims=True)
            p = jnp.exp2((s - top) * factor).astype(jnp.bfloat16)
            o = jnp.dot(p, vc[...], preferred_element_type=jnp.float32)
            o = o[:, 0:HD] / o[:, HD:]
            for h in range(8):
                merged[pl.ds(b * BLK, BLK), pl.ds(g * 1024 + h * HD, HD)] = o[h * BLK:(h + 1) * BLK].astype(jnp.bfloat16)
        for half in range(2):
            unit = b * 2 + half
            to = unit // 3
            source = merged.at[pl.ds(unit * 32, 32)]
            target = out.at[pl.ds((unit % 3) * 32, 32), pl.ds(pl.multiple_of(me * 2048, 2048), 2048)]

            @pl.when(to == me)
            def _():
                pltpu.make_async_copy(source, target, own_sem).start()

            @pl.when(to != me)
            def _():
                pltpu.make_async_remote_copy(
                    src_ref=source, dst_ref=target, send_sem=send_sem, recv_sem=recv_sem,
                    device_id={"head": to}, device_id_type=MESH,
                ).start()
        return carry

    lax.fori_loop(0, 6, one_block, 0)
    most = over[...]
    for r, copy in enumerate(told):
        copy.wait()
        most = jnp.maximum(most, overs[r + 1])
    over_out[...] = most
    pltpu.make_async_copy(out.at[:, pl.ds(0, 2048)], out.at[:, pl.ds(0, 2048)], own_sem).wait()
    pltpu.make_async_copy(out.at[:, pl.ds(0, 6144)], out.at[:, pl.ds(0, 6144)], send_sem).wait()
    pltpu.make_async_copy(out.at[:, pl.ds(0, 6144)], out.at[:, pl.ds(0, 6144)], recv_sem).wait()


def attend_all(number, where, counts, over, queries, k, v):
    smem, vmem = pl.BlockSpec(memory_space=pltpu.SMEM), pl.BlockSpec(memory_space=pltpu.VMEM)
    dma = pltpu.SemaphoreType.DMA
    return pl.pallas_call(
        attend_kernel,
        out_shape=(jax.ShapeDtypeStruct((96, 8192), jnp.bfloat16), jax.ShapeDtypeStruct((1, 128), jnp.int32)),
        in_specs=[smem, smem, vmem, vmem, vmem, vmem],
        out_specs=(pl.BlockSpec(memory_space=pl.ANY), vmem),
        scratch_shapes=[
            pltpu.VMEM((384, 2048), jnp.bfloat16),
            pltpu.VMEM((BLK * 16, HD), jnp.float32),
            pltpu.VMEM((SEL * BLK, HD), jnp.bfloat16),
            pltpu.VMEM((SEL * BLK, 2 * HD), jnp.bfloat16),
            pltpu.VMEM((4, 1, 128), jnp.int32),
            dma, dma, dma, dma((4,)), dma((4,)),
        ],
        compiler_params=pltpu.CompilerParams(
            collective_id=number, has_side_effects=True, vmem_limit_bytes=60 * 2**20
        ),
        name="attend",
    )(where, counts, over, queries, k, v)


def own_requests(blocks, counts):
    me = lax.axis_index("ctx")
    z = me // NW
    flat = blocks.reshape(-1)
    ids = np.arange(ITEMS * SEL)
    live = (jnp.asarray(ids % SEL)[None, :].reshape(ITEMS, SEL) < counts.reshape(ITEMS, 1)).reshape(-1)
    holder = jnp.where(live, flat // BLK, -1)
    earlier = jnp.asarray(ids[None, :] < ids[:, None])
    rank = jnp.sum(((holder[:, None] == holder[None, :]) & earlier).astype(jnp.int32), axis=1)
    core = holder % 2
    lane = (holder // 2 % 4) * 2 + (rank + core) % 2
    away = (z - holder // NW + NZ) % NZ
    inside = core * 3 + rank // 2
    tile = core * 128 + jnp.asarray(ids // SEL % 2) * BLK + flat % BLK + 1
    slot = jnp.where(live, lane * 48 + away * 6 + inside, -1)
    mine = jnp.sum(jnp.where(slot[None, :] == jnp.arange(NW * 48)[:, None], tile[None, :], 0), axis=1)
    mine = jnp.pad(mine.reshape(NW, 1, 48), ((0, 0), (0, 0), (0, 80)))
    where = jnp.where(live, away * 48 + lane * 6 + inside, 0)
    return mine, where


def plan(table, caps):
    asked = table.reshape(NZ, NW, 128)[:, :, :48].reshape(NZ, NW, NZ, 6)
    by_k = [jnp.roll(asked[:, :, k], -k, axis=0) for k in range(NZ)]
    up = [by_k[4][:, 0::2], by_k[3], by_k[2], by_k[1]]
    down = [by_k[4][:, 1::2], by_k[5], by_k[6], by_k[7]]
    lists = jnp.stack([jnp.concatenate([e.reshape(NZ, -1) for e in way], axis=1) for way in (up, down)])
    live = lists > 0
    size = lists.shape[2]
    before = jnp.asarray(np.triu(np.ones((size, size), np.float32), 1))
    at = jnp.dot(live.reshape(-1, size).astype(jnp.float32), before).astype(jnp.int32).reshape(lists.shape)
    hit = (at[:, 0, None, :] == jnp.arange(caps[0])[None, :, None]) & live[:, 0, None, :]
    src = jnp.maximum(jnp.sum(jnp.where(hit, lists[:, 0, None, :], 0), axis=2) - 1, 0)
    ends = np.cumsum([24, 48, 48, 48])
    totals = [jnp.sum(live[:, :, :e].astype(jnp.int32), axis=2) for e in ends]
    over = jnp.stack([jnp.max(t) > c for t, c in zip(totals, caps[::-1])]).any()

    def seg(d, k, part):
        lo, hi = (0, 24) if part == 0 else (24 + 48 * (part - 1), 24 + 48 * part)
        return jnp.minimum(at[d, (NZ - k) % NZ, lo:hi], caps[3 - part] - 1)

    here = jnp.maximum(by_k[0][0].reshape(-1) - 1, 0)
    four = jnp.stack([seg(0, 4, 0).reshape(4, 6), seg(1, 4, 0).reshape(4, 6)], axis=1).reshape(-1)
    post = jnp.concatenate(
        [here, seg(0, 1, 3), seg(0, 2, 2), seg(0, 3, 1), four, seg(1, 5, 1), seg(1, 6, 2), seg(1, 7, 3)]
    )
    return src.reshape(-1), post, over


def per_device(queries, keys, values, sel_blocks, sel_counts):
    k_own = keys.reshape(128, BLK, HD)
    v_own = values.reshape(128, BLK, HD)
    mine, where = own_requests(sel_blocks, sel_counts)
    counts = sel_counts.reshape(-1)
    table, k_twin = exchange_requests(mine, k_own)
    src, post, over = plan(table, USUAL)
    over = jnp.broadcast_to(over.astype(jnp.int32), (1, 128))
    k, v, over = exchange_tiles(1, USUAL, src, post, over, (k_own, v_own), (k_twin, None))
    out, over = attend_all(2, where, counts, over, queries, k, v)

    def again():
        src, post, _ = plan(table, FULL)
        none = jnp.zeros((1, 128), jnp.int32)
        k, _ = exchange_tiles(3, FULL, src, post, none, (k_own,), (None,))
        v, _ = exchange_tiles(4, FULL, src, post, none, (v_own,), (None,))
        return attend_all(5, where, counts, none, queries, k, v)[0]

    return lax.cond(over[0, 0] > 0, again, lambda: out)


def solution(mesh):
    placed = (
        P("ctx", "head", None),
        P("head", "ctx", None),
        P("head", "ctx", None),
        P("ctx", "head", None),
        P("ctx", "head"),
    )
    return jax.shard_map(
        per_device, mesh=mesh, in_specs=placed, out_specs=P(("ctx", "head"), None), check_vma=False
    )
```

time: 439 us -> 291 us (0.66); the launches traced: 434 us -> 290 us
  Pallas kernels: 0 us -> 273 us
  blocking collectives: 188 us -> 0 us
  waiting for transfers between devices: 132 us -> 0 us
  matrix products: 45.6 us -> 0.13 us
  local copies, waits for them, and re-layouts: 39.1 us -> 7.77 us
  other arithmetic: 21.4 us -> 6.26 us
  starting transfers between devices: 7.43 us -> 0 us
    pallas_call x0 -> x3, Pallas kernels: none -> 273 us  [the longest x1 222 us: exchange_tiles(): pl.pallas_call(lambda *refs: tiles_kernel(caps, n, fetch, *refs), out_sha...]
    all_to_all x3 -> x0, blocking collectives: 188 us -> none  [the longest x1 144 us: per_device(): lax.all_to_all(key_out, 'ctx', split_axis=0, concat_axis=0, tiled=True)]
    all_to_all x1 -> x0, waiting for transfers between devices: 132 us -> none  [per_device(): lax.all_to_all(value_out, 'ctx', split_axis=0, concat_axis=0, tiled=True)]
    dot_general x24 -> x1, matrix products: 45.6 us -> 0.13 us  [plan(): jnp.dot(live.reshape(-1, size).astype(jnp.float32), before)]
    gather x4 -> x0, local copies, waits for them, and re-layouts: 29.9 us -> none  [the longest x1 13.3 us: per_device(): key_out = jnp.take(key_table, tile_ids, axis=0)]
    select_n x5 -> x2, other arithmetic: 13.4 us -> 0.03 us  [the longest x1 0.03 us: own_requests(): slot = jnp.where(live, lane * 48 + away * 6 + inside, -1)]
    all_to_all x1 -> x0, starting transfers between devices: 7.43 us -> none  [per_device(): lax.all_to_all(value_out, 'ctx', split_axis=0, concat_axis=0, tiled=True)]
    reduce_sum x14 -> x7, other arithmetic: 7.11 us -> 1.9 us  [the longest x1 0.99 us: own_requests(): jnp.sum(((holder[:, None] == holder[None, :]) & earlier).astype(jnp.int32...]
  transfers between devices with their start and end apart: 1 -> 0, of which waited for: 1 -> 0; matrix products, arithmetic and copies ran while one was open for 2% -> 0% of each run, Pallas kernels for 0% -> 0%
where the time goes in v1:
time: 291 us; the launch traced here: 290 us
  Pallas kernels  273 us (94%)
  local copies, waits for them, and re-layouts  7.77 us (3%)
  other arithmetic  6.26 us (2%)
  between operations  3.42 us (1%)
    pallas_call x1, Pallas kernels, exchange_tiles(): pl.pallas_call(lambda *refs: tiles_kernel(caps, n, fetch, *refs), out_sha...  222 us
    pallas_call x1, Pallas kernels, attend_all(): pl.pallas_call(attend_kernel, out_shape=(jax.ShapeDtypeStruct((96, 8192),...  33.4 us
    pallas_call x1, Pallas kernels, exchange_requests(): pl.pallas_call(requests_kernel, out_shape=(jax.ShapeDtypeStruct((NZ * NW,...  16.7 us

profile of v1, /device:TPU:1, one launch (start us, length us, event | category | flops | bytes accessed | tf_op | source)
XLA Modules:
  0.0 290.3 jit_solution(2968231709444094848)
XLA Ops:
  0.0 0.9 reshape.259
  0.9 0.8 copy.26
  1.7 0.1 lt.35.counts
  1.8 0.8 broadcast_compare_fusion
  2.5 0.1 reshape.270
  2.6 0.7 fusion.29
  3.3 1.0 convert_reduce_fusion
  4.4 0.1 select_reduce_fusion.1
  4.5 0.1 reshape.260
  4.6 0.6 pad.4.mine
  5.2 16.7 %requests.1 = (s32[64,1,128]{2,1,0:T(1,128)S(1)}, bf16[128,64,128]{2,1,0:T(8,128)(2,1)}) custom-call(s32[8,1,128]{2,1,0:T(1,128)} %pad.4.mine, bf16[128,64,128]{2,1,0:T(8,128)(2,1)} %bitcast.80), custom_call_target="tpu_custom_call" | custom-call | tf_op jit(solution)/shard_map/requests/pallas_call | solution.py:71
  21.9 0.1 reshape.263
  22.1 0.1 max.33
  22.2 0.1 concatenate.144
  22.3 0.1 concatenate.135
  22.4 0.1 concatenate.141
  22.5 0.1 concatenate.132
  22.7 0.1 concatenate.138
  22.7 0.1 concatenate.129
  22.9 0.1 reshape.264
  23.0 0.1 reshape.265
  23.1 0.1 slice_reduce_fusion.16
  23.4 0.1 slice_reduce_fusion.14
  23.5 0.2 slice_reduce_fusion.12
  23.7 0.1 concatenate.145
  23.8 0.1 concatenate.142
  24.0 0.1 add_bitcast_fusion.2
  24.1 0.1 convert_reduce_fusion.1
  24.3 0.6 reduce_max.39
  25.6 0.1 convert_reduce_fusion.2
  25.7 0.6 reduce_max.38
  27.0 0.1 convert_reduce_fusion.3
  27.2 0.6 reduce_max.37
  28.5 0.1 convert_reduce_fusion.4
  28.6 0.6 reduce_max.36
  29.9 0.5 broadcast_in_dim.59.refs_2_
  30.4 0.1 fusion.15
  30.6 0.1 min.131
  30.7 0.1 min.133
  30.8 0.1 reshape.267
  30.9 0.1 fusion.31
  31.0 0.7 concatenate.148.refs_1_
  31.6 0.2 select_reduce_fusion.2
  31.9 0.7 max.31.refs_0_
  32.5 222.3 %tiles.5 = (bf16[384,64,128]{2,1,0:T(8,128)(2,1)}, bf16[384,64,128]{2,1,0:T(8,128)(2,1)}, s32[1,128]{1,0:T(1,128)}) custom-call(s32[216]{0:T(256)} %max.31.refs_0_, s32[384]{0:T(512)} %concatenate.148.refs_1_, s32[1,128]{1,0:T(1,128)} %broadcast_in_dim.59.refs_2_, bf16[128,64,128]{2,1,0:T(8,128)(2,1)S(1)} %bitcast.81, bf16[128,64,128]{2,1,0:T(8,128)(2,1)} %bitcast.83, ...), custom_call_target="tpu_custom_call" | custom-call | tf_op jit(solution)/shard_map/tiles/pallas_call | solution.py:264
  254.9 33.4 %attend.3 = (bf16[96,8192]{1,0:T(8,128)(2,1)S(1)}, s32[1,128]{1,0:T(1,128)}) custom-call(s32[192]{0:T(256)S(1)} %add_select_fusion.1.where, s32[12]{0:T(128)S(1)} %lt.35.counts, s32[1,128]{1,0:T(1,128)} %get-tuple-element.42.over, bf16[384,16,128]{2,1,0:T(8,128)(2,1)} %q.1, bf16[384,64,128]{2,1,0:T(8,128)(2,1)} %get-tuple-element.43.k, ...), custom_call_target="tpu_custom_call" | custom-call | tf_op jit(solution)/shard_map/attend/pallas_call | solution.py:361
  288.9 0.2 conditional.1
  289.1 1.1 copy.54
  (27 shorter events, 0.7 us)
Async XLA Ops:
  0.0 30.4 %copy-start.1 = (bf16[168,168]{1,0:T(8,128)(2,1)S(1)}, bf16[168,168]{1,0:T(8,128)(2,1)}, u32[]{:S(2)}) copy-start(bf16[168,168]{1,0:T(8,128)(2,1)} %constant.364) | copy-start | bytes 169348
  0.0 32.5 %copy-start = (bf16[2,4096,128]{2,1,0:T(8,128)(2,1)S(1)}, bf16[2,4096,128]{2,1,0:T(8,128)(2,1)}, u32[]{:S(2)}) copy-start(bf16[2,4096,128]{2,1,0:T(8,128)(2,1)} %param.13) | copy-start | bytes 6291460

commit v2 on v1

--- a/solution.py
+++ b/solution.py
@@ -13,7 +13,7 @@
 NZ = 8
 NW = 8
 STEPS = 4
-USUAL = (108, 84, 56, 24)
+USUAL = (104, 78, 50, 24)
 FULL = (168, 120, 72, 24)
 MESH = pl.DeviceIdType.MESH
 
@@ -22,7 +22,11 @@
     return {"ctx": index}
 
 
-def requests_kernel(mine, k_own, table, k_twin, local_sem, send_sem, recv_sem):
+def requests_kernel(
+    mine, kinds, within, same, lower, column, k_own,
+    table, src, post, over, k_twin,
+    rows, local_sem, send_sem, recv_sem,
+):
     me = lax.axis_index("ctx")
     z, w = me // NW, me % NW
     barrier = pltpu.get_barrier_semaphore()
@@ -31,31 +35,31 @@
         pl.semaphore_signal(barrier, inc=1, device_id=at_ctx((z + r) % NZ * NW + w), device_id_type=MESH)
     pl.semaphore_wait(barrier, 14)
 
-    own = pltpu.make_async_copy(mine.at[pl.ds(w, 1)], table.at[pl.ds(w, 1)], local_sem)
+    own = pltpu.make_async_copy(mine.at[pl.ds(w, 1)], rows.at[pl.ds(w, 1)], local_sem)
     own.start()
     inside = []
     for r in range(1, NW):
         ow = (w + r) % NW
         copy = pltpu.make_async_remote_copy(
-            src_ref=mine.at[pl.ds(ow, 1)], dst_ref=table.at[pl.ds(w, 1)],
+            src_ref=mine.at[pl.ds(ow, 1)], dst_ref=rows.at[pl.ds(w, 1)],
             send_sem=send_sem.at[r], recv_sem=recv_sem.at[r],
             device_id=at_ctx(z * NW + ow), device_id_type=MESH,
         )
         copy.start()
         inside.append(copy)
-    twin = me + 1 - 2 * (me % 2)
     keys_over = pltpu.make_async_remote_copy(
         src_ref=k_own, dst_ref=k_twin, send_sem=send_sem.at[0], recv_sem=recv_sem.at[0],
-        device_id=at_ctx(twin), device_id_type=MESH,
+        device_id=at_ctx(me + 1 - 2 * (me % 2)), device_id_type=MESH,
     )
     keys_over.start()
     own.wait()
     for copy in inside:
         copy.wait()
+    table[0] = jnp.concatenate([rows[i] for i in range(NW)], axis=0)
     along = []
     for r in range(1, NZ):
         copy = pltpu.make_async_remote_copy(
-            src_ref=table.at[pl.ds(0, NW)], dst_ref=table.at[pl.ds((NZ - r) * NW, NW)],
+            src_ref=table.at[0], dst_ref=table.at[NZ - r],
             send_sem=send_sem.at[NW + r], recv_sem=recv_sem.at[NW + r],
             device_id=at_ctx((z + r) % NZ * NW + w), device_id_type=MESH,
         )
@@ -63,27 +67,99 @@
         along.append(copy)
     for copy in along:
         copy.wait()
+
+    kind = kinds[...]
+    asked = [table[i] for i in range(NZ)]
+    by_source = []
+    for i in range(NZ):
+        row = jnp.zeros((NW, 128), jnp.int32)
+        for k in range(NZ):
+            row = jnp.where(kind == k, asked[(i + k) % NZ], row)
+        by_source.append(row)
+    tiles = jnp.concatenate(by_source, axis=0)
+    kind = jnp.concatenate([kind] * NZ, axis=0)
+    live = tiles > 0
+    ones = live.astype(jnp.float32)
+    dot = lambda x, y: jnp.dot(x, y, preferred_element_type=jnp.float32)
+    per_row = dot(ones, same[...])
+    at = dot(ones, within[...]) + dot(lower[...], per_row)
+    sums = dot(column[...], per_row)
+    n = [sums[:, 6 * k:6 * k + 1] for k in range(NZ)]
+    c1, c2, c3, c4 = (float(c) for c in USUAL)
+    least = lambda x, y, t: jnp.minimum(
+        jnp.minimum(jnp.full_like(x, c4), c3 - x), jnp.minimum(c2 - x - y, c1 - x - y - t)
+    )
+    room_up, room_down = least(n[3], n[2], n[1]), least(n[5], n[6], n[7])
+    four_up = jnp.clip(room_up, 0.0, n[4])
+    four_down = n[4] - four_up
+    short = (room_up < 0) | (room_down < 0) | (four_down > room_down)
+    over[...] = jnp.broadcast_to(jnp.max(short.astype(jnp.float32), axis=0, keepdims=True), (1, 128)).astype(jnp.int32)
+    up = (kind < 4) | ((kind == 4) & (at < four_up))
+    base = jnp.zeros_like(at)
+    for k, first in (
+        (3, four_up), (2, four_up + n[3]), (1, four_up + n[3] + n[2]),
+        (5, four_down), (6, four_down + n[5]), (7, four_down + n[5] + n[6]),
+    ):
+        base = jnp.where(kind == k, first, base)
+    base = jnp.where((kind == 4) & (at >= four_up), -four_up, base)
+    at = at + base
+
+    places = lax.broadcasted_iota(jnp.int32, (128, 128), 0).astype(jnp.float32)
+    found = []
+    for way in range(2):
+        mine_too = live[0:NW] & (up[0:NW] if way == 0 else ~up[0:NW]) & (kind[0:NW] > 0)
+        place = jnp.where(mine_too, at[0:NW], -1.0)
+        value = jnp.where(mine_too, tiles[0:NW], 0).astype(jnp.float32)
+        total = jnp.zeros((128, 128), jnp.float32)
+        for i in range(NW):
+            total = jnp.where(place[i:i + 1] == places, value[i:i + 1], total)
+        found.append(
+            lax.dot_general(
+                jnp.ones((8, 128), jnp.float32), total, (((1,), (1,)), ((), ())), preferred_element_type=jnp.float32
+            )
+        )
+    row = lax.broadcasted_iota(jnp.int32, (8, 128), 0)
+    src[...] = jnp.maximum(jnp.where(row == 0, found[0], found[1]).astype(jnp.int32) - 1, 0)
+
+    cap = jnp.full((NZ * NW, 128), c1)
+    for k in range(2, 7):
+        cap = jnp.where(kind == k, (c1, c2, c3, c4)[min(k, NZ - k) - 1], cap)
+    spot = jnp.clip(at, 0.0, cap - 1) + jnp.where(up, 0.0, cap)
+    spot = spot.astype(jnp.int32)
+    mine_at = jnp.maximum(tiles[0:NW] - 1, 0)
+    for k in range(1, NZ):
+        i = NZ - k
+        mine_at = jnp.where(kind[0:NW] == k, spot[i * NW:(i + 1) * NW], mine_at)
+    post[...] = mine_at
     keys_over.wait()
 
 
 def exchange_requests(mine, k_own):
     vmem, anywhere = pl.BlockSpec(memory_space=pltpu.VMEM), pl.BlockSpec(memory_space=pl.ANY)
+    lane, row = np.arange(128), np.arange(NZ * NW)
+    block = (lane[:, None] // 6 == lane[None, :] // 6) & (lane[:, None] < 48)
+    plane = row[:, None] // NW == row[None, :] // NW
+    kinds = np.broadcast_to(np.where(lane < 48, lane // 6, 9), (NW, 128)).astype(np.int32)
+    within = (block & (lane[:, None] < lane[None, :])).astype(np.float32)
+    lower = (plane & (row[None, :] < row[:, None])).astype(np.float32)
+    ints = lambda *shape: jax.ShapeDtypeStruct(shape, jnp.int32)
     return pl.pallas_call(
         requests_kernel,
         out_shape=(
-            jax.ShapeDtypeStruct((NZ * NW, 1, 128), jnp.int32),
+            ints(NZ, NW, 128), ints(8, 128), ints(NW, 128), ints(1, 128),
             jax.ShapeDtypeStruct(k_own.shape, k_own.dtype),
         ),
-        in_specs=[vmem, anywhere],
-        out_specs=(vmem, anywhere),
+        in_specs=[*[vmem] * 6, anywhere],
+        out_specs=(*[vmem] * 4, anywhere),
         scratch_shapes=[
+            pltpu.VMEM((NW, 1, 128), jnp.int32),
             pltpu.SemaphoreType.DMA,
             pltpu.SemaphoreType.DMA((16,)),
             pltpu.SemaphoreType.DMA((16,)),
         ],
         compiler_params=pltpu.CompilerParams(collective_id=0, has_side_effects=True),
         name="requests",
-    )(mine, k_own)
+    )(mine, kinds, within, block.astype(np.float32), lower, plane.astype(np.float32), k_own)
 
 
 def tiles_kernel(caps, arrays, fetch, src, post, over, *refs):
@@ -141,8 +217,8 @@
         source = lists[a] if step == 1 else hops[a][step - 2]
         number = (0, 4, 7, 9)[step - 1] + piece
         return pltpu.make_async_remote_copy(
-            src_ref=source.at[d, pl.ds(lo, hi - lo)],
-            dst_ref=hops[a][step - 1].at[d, pl.ds(lo, hi - lo)],
+            src_ref=source.at[pl.ds(d * caps[max(step - 2, 0)] + lo, hi - lo)],
+            dst_ref=hops[a][step - 1].at[pl.ds(d * caps[step - 1] + lo, hi - lo)],
             send_sem=z_send.at[a, d, number],
             recv_sem=z_recv.at[a, d, number],
             device_id=at_ctx(towards[d]),
@@ -152,35 +228,21 @@
     def pack(a, piece):
         for d in range(2):
             def one(i, carry):
-                lists[a][d, i] = tab[a][src[d * caps[0] + i]]
+                lists[a][d * caps[0] + i] = tab[a][src[d, i]]
                 return carry
 
             lax.fori_loop(cuts[piece], cuts[piece + 1], one, 0)
 
     def deliver(a, k):
         base = k * NW * 6
-        if k == 4:
-            def both(i, carry):
-                at = base + i
-                for d in range(2):
-                    for s in range(6):
-                        stage[a][base + (2 * i + d) * 6 + s] = hops[a][3][d, post[base + (2 * i + d) * 6 + s]]
-                return carry
-
-            lax.fori_loop(0, NW // 2, both, 0)
-        else:
-            def one(i, carry):
-                index = post[base + i]
-                if k == 0:
-                    tile = tab[a][index]
-                elif k < 4:
-                    tile = hops[a][k - 1][0, index]
-                else:
-                    tile = hops[a][7 - k][1, index]
-                stage[a][base + i] = tile
-                return carry
-
-            lax.fori_loop(0, NW * 6, one, 0)
+        source = tab[a] if k == 0 else hops[a][min(k, NZ - k) - 1]
+
+        def one(i, carry):
+            for j in range(6):
+                stage[a][base + i * 6 + j] = source[post[i, k * 6 + j]]
+            return carry
+
+        lax.fori_loop(0, NW, one, 0)
 
         def send(r, carry):
             ow = (w + r) % NW
@@ -268,9 +330,9 @@
         out_specs=(*[anywhere] * n, whole),
         scratch_shapes=[
             *[vmem(256)] * n,
-            *[vmem(2, caps[0])] * n,
+            *[vmem(2 * caps[0])] * n,
             *[vmem(NZ * NW * 6)] * n,
-            *[vmem(2, c) for c in caps] * n,
+            *[vmem(2 * c) for c in caps] * n,
             pltpu.VMEM((NW, 1, 128), jnp.int32),
             dma((n, 2)), dma((n,)), dma((n, 2, 10)), dma((n, 2, 10)),
             dma((n,)), dma((n,)), dma((n,)), dma((NW,)), dma((NW,)),
@@ -399,8 +461,8 @@
     return mine, where
 
 
-def plan(table, caps):
-    asked = table.reshape(NZ, NW, 128)[:, :, :48].reshape(NZ, NW, NZ, 6)
+def full_plan(table):
+    asked = table[:, :, :48].reshape(NZ, NW, NZ, 6)
     by_k = [jnp.roll(asked[:, :, k], -k, axis=0) for k in range(NZ)]
     up = [by_k[4][:, 0::2], by_k[3], by_k[2], by_k[1]]
     down = [by_k[4][:, 1::2], by_k[5], by_k[6], by_k[7]]
@@ -409,22 +471,17 @@
     size = lists.shape[2]
     before = jnp.asarray(np.triu(np.ones((size, size), np.float32), 1))
     at = jnp.dot(live.reshape(-1, size).astype(jnp.float32), before).astype(jnp.int32).reshape(lists.shape)
-    hit = (at[:, 0, None, :] == jnp.arange(caps[0])[None, :, None]) & live[:, 0, None, :]
+    hit = (at[:, 0, None, :] == jnp.arange(size)[None, :, None]) & live[:, 0, None, :]
     src = jnp.maximum(jnp.sum(jnp.where(hit, lists[:, 0, None, :], 0), axis=2) - 1, 0)
-    ends = np.cumsum([24, 48, 48, 48])
-    totals = [jnp.sum(live[:, :, :e].astype(jnp.int32), axis=2) for e in ends]
-    over = jnp.stack([jnp.max(t) > c for t, c in zip(totals, caps[::-1])]).any()
 
     def seg(d, k, part):
         lo, hi = (0, 24) if part == 0 else (24 + 48 * (part - 1), 24 + 48 * part)
-        return jnp.minimum(at[d, (NZ - k) % NZ, lo:hi], caps[3 - part] - 1)
-
-    here = jnp.maximum(by_k[0][0].reshape(-1) - 1, 0)
-    four = jnp.stack([seg(0, 4, 0).reshape(4, 6), seg(1, 4, 0).reshape(4, 6)], axis=1).reshape(-1)
-    post = jnp.concatenate(
-        [here, seg(0, 1, 3), seg(0, 2, 2), seg(0, 3, 1), four, seg(1, 5, 1), seg(1, 6, 2), seg(1, 7, 3)]
-    )
-    return src.reshape(-1), post, over
+        return jnp.minimum(at[d, (NZ - k) % NZ, lo:hi], FULL[3 - part] - 1) + d * FULL[3 - part]
+
+    here = jnp.maximum(by_k[0][0] - 1, 0)
+    four = jnp.stack([seg(0, 4, 0).reshape(4, 6), seg(1, 4, 0).reshape(4, 6)], axis=1)
+    parts = [here, seg(0, 1, 3), seg(0, 2, 2), seg(0, 3, 1), four, seg(1, 5, 1), seg(1, 6, 2), seg(1, 7, 3)]
+    return src, jnp.concatenate([p.reshape(NW, 6) for p in parts], axis=1)
 
 
 def per_device(queries, keys, values, sel_blocks, sel_counts):
@@ -432,14 +489,12 @@
     v_own = values.reshape(128, BLK, HD)
     mine, where = own_requests(sel_blocks, sel_counts)
     counts = sel_counts.reshape(-1)
-    table, k_twin = exchange_requests(mine, k_own)
-    src, post, over = plan(table, USUAL)
-    over = jnp.broadcast_to(over.astype(jnp.int32), (1, 128))
+    table, src, post, over, k_twin = exchange_requests(mine, k_own)
     k, v, over = exchange_tiles(1, USUAL, src, post, over, (k_own, v_own), (k_twin, None))
     out, over = attend_all(2, where, counts, over, queries, k, v)
 
     def again():
-        src, post, _ = plan(table, FULL)
+        src, post = full_plan(table)
         none = jnp.zeros((1, 128), jnp.int32)
         k, _ = exchange_tiles(3, FULL, src, post, none, (k_own,), (None,))
         v, _ = exchange_tiles(4, FULL, src, post, none, (v_own,), (None,))

time: 291 us -> 275 us (0.945)
  Pallas kernels: 273 us -> 267 us
  local copies, waits for them, and re-layouts: 7.77 us -> 3.7 us
  other arithmetic: 6.26 us -> 2.63 us
    pallas_call x1, Pallas kernels: 222 us -> 215 us  [exchange_tiles(): pl.pallas_call(lambda *refs: tiles_kernel(caps, n, fetch, *refs), out_sha...]
where the time goes in v2:
time: 275 us; the launch traced here: 274 us
  Pallas kernels  267 us (97%)
  local copies, waits for them, and re-layouts  3.7 us (1%)
    pallas_call x1, Pallas kernels, exchange_tiles(): pl.pallas_call(lambda *refs: tiles_kernel(caps, n, fetch, *refs), out_sha...  215 us
    pallas_call x1, Pallas kernels, attend_all(): pl.pallas_call(attend_kernel, out_shape=(jax.ShapeDtypeStruct((96, 8192),...  33.4 us
    pallas_call x1, Pallas kernels, exchange_requests(): pl.pallas_call(requests_kernel, out_shape=(ints(NZ, NW, 128), ints(8, 128...  18.4 us

profile of v2, /device:TPU:1, one launch (start us, length us, event | category | flops | bytes accessed | tf_op | source)
XLA Modules:
  0.0 274.2 jit_solution(16624364423960956319)
XLA Ops:
  0.0 0.0 copy-start
  0.0 0.9 reshape.155
  0.9 0.8 copy.28
  1.7 0.1 lt.35.counts
  1.8 0.8 broadcast_compare_fusion
  2.5 0.1 reshape.165
  2.6 0.7 fusion.25
  3.3 1.0 convert_reduce_fusion
  4.4 0.1 select_reduce_fusion.1
  4.5 0.1 reshape.156
  4.6 0.6 pad.4.mine
  5.2 18.4 %requests.1 = (s32[8,8,128]{2,1,0:T(8,128)S(1)}, s32[8,128]{1,0:T(8,128)}, s32[8,128]{1,0:T(8,128)}, s32[1,128]{1,0:T(1,128)}, bf16[128,64,128]{2,1,0:T(8,128)(2,1)}) custom-call(s32[8,1,128]{2,1,0:T(1,128)} %pad.4.mine, s32[8,128]{1,0:T(8,128)} %constant.165.clone.kinds, f32[128,128]{1,0:T(8,128)} %constant.166.clone.within, ...), custom_call_target="tpu_custom_call" | custom-call | tf_op jit(solution)/shard_map/requests/pallas_call | solution.py:146
  23.6 0.0 copy-done
  23.6 215.3 %tiles.3 = (bf16[384,64,128]{2,1,0:T(8,128)(2,1)}, bf16[384,64,128]{2,1,0:T(8,128)(2,1)}, s32[1,128]{1,0:T(1,128)}) custom-call(s32[8,128]{1,0:T(8,128)} %get-tuple-element.43.refs_0_, s32[8,128]{1,0:T(8,128)} %get-tuple-element.44.refs_1_, s32[1,128]{1,0:T(1,128)} %get-tuple-element.45.refs_2_, bf16[128,64,128]{2,1,0:T(8,128)(2,1)S(1)} %bitcast.31, ...), custom_call_target="tpu_custom_call" | custom-call | tf_op jit(solution)/shard_map/tiles/pallas_call | solution.py:326
  238.8 33.4 %attend.2 = (bf16[96,8192]{1,0:T(8,128)(2,1)S(1)}, s32[1,128]{1,0:T(1,128)}) custom-call(s32[192]{0:T(256)S(1)} %add_select_fusion.1.where, s32[12]{0:T(128)S(1)} %lt.35.counts, s32[1,128]{1,0:T(1,128)} %get-tuple-element.47.over, bf16[384,16,128]{2,1,0:T(8,128)(2,1)} %q.1, bf16[384,64,128]{2,1,0:T(8,128)(2,1)} %get-tuple-element.48.k, ...), custom_call_target="tpu_custom_call" | custom-call | tf_op jit(solution)/shard_map/attend/pallas_call | solution.py:423
  272.9 0.2 conditional.1
  273.1 1.1 copy.43
  (2 shorter events, 0.0 us)
Async XLA Ops:
  0.0 23.6 %copy-start = (bf16[2,4096,128]{2,1,0:T(8,128)(2,1)S(1)}, bf16[2,4096,128]{2,1,0:T(8,128)(2,1)}, u32[]{:S(2)}) copy-start(bf16[2,4096,128]{2,1,0:T(8,128)(2,1)} %param.17) | copy-start | bytes 6291460

commit v3 on v2

--- a/solution.py
+++ b/solution.py
@@ -440,6 +440,301 @@
     )(where, counts, over, queries, k, v)
 
 
+def fused_kernel(
+    src, post, where, counts, over, q_in, k_own, v_own, k_twin, out, over_out,
+    tab_k, tab_v, packed, stage, k1, k2, k3, k4, v1, v2, v3, v4, land_k, land_v, more,
+    q, merged, qf, kc, vc, overs, overs_head,
+    q_sem, tab_sem, twin_send, z_send, z_recv, y_send, y_recv, y_local,
+    over_send, over_recv, out_send, out_recv, out_own,
+):
+    caps = USUAL
+    cuts = (0, *caps[::-1])
+    tab, land, hops = (tab_k, tab_v), (land_k, land_v), ((k1, k2, k3, k4), (v1, v2, v3, v4))
+    me = lax.axis_index("ctx")
+    head = lax.axis_index("head")
+    z, w = me // NW, me % NW
+    core = me % 2
+    towards = (((z + 1) % NZ) * NW + w, ((z + NZ - 1) % NZ) * NW + w)
+
+    barrier = pltpu.get_barrier_semaphore()
+    for other in towards:
+        pl.semaphore_signal(barrier, inc=1, device_id=at_ctx(other), device_id_type=MESH)
+    for r in range(1, NW):
+        pl.semaphore_signal(barrier, inc=1, device_id=at_ctx(z * NW + (w + r) % NW), device_id_type=MESH)
+    for r in range(1, 4):
+        pl.semaphore_signal(barrier, inc=1, device_id={"head": (head + r) % 4}, device_id_type=MESH)
+    pl.semaphore_wait(barrier, NW + 4)
+
+    mine_k, mine_v = (t.at[pl.ds(core * 128, 128)] for t in tab)
+    twin_k = tab_k.at[pl.ds((1 - core) * 128, 128)]
+    loads = (
+        (pltpu.make_async_copy(k_own, mine_k, tab_sem.at[0, 0]), pltpu.make_async_copy(k_twin, twin_k, tab_sem.at[0, 1])),
+        (
+            pltpu.make_async_copy(v_own, mine_v, tab_sem.at[1, 0]),
+            pltpu.make_async_remote_copy(
+                src_ref=v_own, dst_ref=mine_v, send_sem=twin_send, recv_sem=tab_sem.at[1, 1],
+                device_id=at_ctx(me + 1 - 2 * core), device_id_type=MESH,
+            ),
+        ),
+    )
+    for pair in loads:
+        for copy in pair:
+            copy.start()
+    q_load = pltpu.make_async_copy(q_in, q, q_sem)
+    q_load.start()
+    told = []
+    for r in range(1, NW):
+        copy = pltpu.make_async_remote_copy(
+            src_ref=over, dst_ref=overs.at[r], send_sem=over_send.at[r], recv_sem=over_recv.at[r],
+            device_id=at_ctx(z * NW + (w + r) % NW), device_id_type=MESH,
+        )
+        copy.start()
+        told.append(copy)
+
+    def hop(a, d, step, piece):
+        lo, hi = cuts[piece], cuts[piece + 1]
+        source = packed if step == 1 else hops[a][step - 2]
+        number = (0, 4, 7, 9)[step - 1] + piece
+        return pltpu.make_async_remote_copy(
+            src_ref=source.at[pl.ds(d * caps[max(step - 2, 0)] + lo, hi - lo)],
+            dst_ref=hops[a][step - 1].at[pl.ds(d * caps[step - 1] + lo, hi - lo)],
+            send_sem=z_send.at[a, d, number],
+            recv_sem=z_recv.at[a, d, number],
+            device_id=at_ctx(towards[d]),
+            device_id_type=MESH,
+        )
+
+    def pack_and_start(a):
+        for piece in range(STEPS):
+            for d in range(2):
+                def one(i, carry):
+                    packed[d * caps[0] + i] = tab[a][src[d, i]]
+                    return carry
+
+                lax.fori_loop(cuts[piece], cuts[piece + 1], one, 0)
+                hop(a, d, 1, piece).start()
+
+    def settle(a, k):
+        pltpu.make_async_copy(stage.at[pl.ds(0, 42)], stage.at[pl.ds(0, 42)], y_send.at[a, k]).wait()
+        pltpu.make_async_copy(stage.at[pl.ds(0, 6)], stage.at[pl.ds(0, 6)], y_local.at[a, k]).wait()
+
+    def deliver(a, k):
+        base = k * NW * 6
+        source = tab[a] if k == 0 else hops[a][min(k, NZ - k) - 1]
+        if a and k != STEPS:
+            settle(0, k)
+
+        def one(i, carry):
+            for j in range(6):
+                stage[base + i * 6 + j] = source[post[i, k * 6 + j]]
+            return carry
+
+        lax.fori_loop(0, NW, one, 0)
+
+        def send(r, carry):
+            ow = (w + r) % NW
+            pltpu.make_async_remote_copy(
+                src_ref=stage.at[pl.ds(base + ow * 6, 6)],
+                dst_ref=land[a].at[pl.ds(base + w * 6, 6)],
+                send_sem=y_send.at[a, k],
+                recv_sem=y_recv.at[a],
+                device_id=at_ctx(z * NW + ow),
+                device_id_type=MESH,
+            ).start()
+            return carry
+
+        lax.fori_loop(1, NW, send, 0)
+        pltpu.make_async_copy(
+            stage.at[pl.ds(base + w * 6, 6)], land[a].at[pl.ds(base + w * 6, 6)], y_local.at[a, k]
+        ).start()
+
+    def arrive_and_pass(a, step):
+        for piece in range(5 - step):
+            for d in range(2):
+                hop(a, d, step, piece).wait_recv()
+                if piece < 4 - step:
+                    hop(a, d, step + 1, piece).start()
+
+    def all_landed(a):
+        remote = NZ * (NW - 1) * 6
+        pltpu.make_async_copy(land[a].at[pl.ds(0, remote)], land[a].at[pl.ds(0, remote)], y_recv.at[a]).wait()
+
+    keys = SEL * BLK
+    factor = float(HD ** -0.5 * np.log2(np.e))
+    first = ((head + 1) * 3 // 2) % 6 * 2
+
+    def weigh(ref, n, spot):
+        item = (first + n) % ITEMS
+        b, g = item // 2, item % 2
+        qf[...] = q[pl.ds(b * BLK, BLK)].astype(jnp.float32).reshape(BLK * 16, HD)
+
+        def gather(i, c):
+            kc[pl.ds(i * BLK, BLK)] = land_k[where[item * SEL + i]]
+            return c
+
+        lax.fori_loop(0, SEL, gather, 0)
+        rows = jnp.concatenate(
+            [qf[pl.ds(g * 8 + h, BLK, stride=16)].astype(jnp.bfloat16) for h in range(8)], axis=0
+        )
+        s = lax.dot_general(rows, kc[...], (((1,), (1,)), ((), ())), preferred_element_type=jnp.float32)
+        kept = lax.broadcasted_iota(jnp.int32, (1, keys), 1) < counts[item] * BLK
+        s = jnp.where(kept, s, -jnp.inf)
+        top = jnp.max(s, axis=1, keepdims=True)
+        p = jnp.exp2((s - top) * factor).astype(jnp.bfloat16)
+        for h in range(8):
+            for c in range(8):
+                ref[spot * 64 + h * 8 + c] = p[h * BLK:(h + 1) * BLK, c * HD:(c + 1) * HD]
+
+    def finish(ref, n, spot):
+        item = (first + n) % ITEMS
+        b, g = item // 2, item % 2
+
+        def gather(i, c):
+            vc[pl.ds(i * BLK, BLK), 0:HD] = land_v[where[item * SEL + i]]
+            return c
+
+        lax.fori_loop(0, SEL, gather, 0)
+        p = jnp.concatenate(
+            [jnp.concatenate([ref[spot * 64 + h * 8 + c] for c in range(8)], axis=1) for h in range(8)], axis=0
+        )
+        o = jnp.dot(p, vc[...], preferred_element_type=jnp.float32)
+        o = (o[:, 0:HD] / o[:, HD:]).astype(jnp.bfloat16)
+        for h in range(8):
+            merged[pl.ds(b * BLK, BLK), pl.ds(pl.multiple_of(g * 1024 + h * HD, HD), HD)] = o[h * BLK:(h + 1) * BLK]
+
+        @pl.when(g == 1)
+        def _():
+            for half in range(2):
+                unit = b * 2 + half
+                to = unit // 3
+                source = merged.at[pl.ds(unit * 32, 32)]
+                target = out.at[pl.ds((unit % 3) * 32, 32), pl.ds(pl.multiple_of(head * 2048, 2048), 2048)]
+
+                @pl.when(to == head)
+                def _():
+                    pltpu.make_async_copy(source, target, out_own).start()
+
+                @pl.when(to != head)
+                def _():
+                    pltpu.make_async_remote_copy(
+                        src_ref=source, dst_ref=target, send_sem=out_send, recv_sem=out_recv,
+                        device_id={"head": to}, device_id_type=MESH,
+                    ).start()
+
+    def over_items(work, ref, lo, hi):
+        def one(n, carry):
+            work(ref, n, n - lo)
+            return carry
+
+        lax.fori_loop(lo, hi, one, 0)
+
+    for copy in loads[0]:
+        copy.wait()
+    pack_and_start(0)
+    deliver(0, 0)
+    arrive_and_pass(0, 1)
+    for piece in range(STEPS):
+        for d in range(2):
+            hop(0, d, 1, piece).wait_send()
+    for copy in loads[1]:
+        copy.wait()
+    pack_and_start(1)
+    deliver(1, 0)
+    deliver(0, 1)
+    deliver(0, 7)
+    arrive_and_pass(0, 2)
+    deliver(0, 2)
+    deliver(0, 6)
+    arrive_and_pass(1, 1)
+    deliver(1, 1)
+    deliver(1, 7)
+    arrive_and_pass(0, 3)
+    deliver(0, 3)
+    deliver(0, 5)
+    arrive_and_pass(1, 2)
+    deliver(1, 2)
+    deliver(1, 6)
+    arrive_and_pass(0, 4)
+    deliver(0, 4)
+    for step in range(2, STEPS + 1):
+        for piece in range(STEPS + 1 - step):
+            for d in range(2):
+                hop(0, d, step, piece).wait_send()
+    arrive_and_pass(1, 3)
+    deliver(1, 3)
+    deliver(1, 5)
+    vc[:, HD:] = jnp.ones((keys, HD), jnp.bfloat16)
+    q_load.wait()
+    most = over[...]
+    for r, copy in enumerate(told):
+        copy.wait()
+        most = jnp.maximum(most, overs[r + 1])
+    overs_head[0] = most
+    told = []
+    for r in range(1, 4):
+        copy = pltpu.make_async_remote_copy(
+            src_ref=overs_head.at[0], dst_ref=overs_head.at[r], send_sem=over_send.at[NW + r], recv_sem=over_recv.at[NW + r],
+            device_id={"head": (head + r) % 4}, device_id_type=MESH,
+        )
+        copy.start()
+        told.append(copy)
+    settle(0, STEPS)
+    all_landed(0)
+    over_items(weigh, tab_k, 0, 4)
+    arrive_and_pass(1, 4)
+    deliver(1, 4)
+    over_items(weigh, k1, 4, 7)
+    over_items(weigh, more, 7, ITEMS)
+    for step in range(1, STEPS + 1):
+        for piece in range(STEPS + 1 - step):
+            for d in range(2):
+                hop(1, d, step, piece).wait_send()
+    for k in range(NZ):
+        settle(1, k)
+    all_landed(1)
+    over_items(finish, tab_k, 0, 4)
+    over_items(finish, k1, 4, 7)
+    over_items(finish, more, 7, ITEMS)
+    for r, copy in enumerate(told):
+        copy.wait()
+        most = jnp.maximum(most, overs_head[r + 1])
+    over_out[...] = most
+    pltpu.make_async_copy(out.at[:, pl.ds(0, 2048)], out.at[:, pl.ds(0, 2048)], out_own).wait()
+    pltpu.make_async_copy(out.at[:, pl.ds(0, 6144)], out.at[:, pl.ds(0, 6144)], out_send).wait()
+    pltpu.make_async_copy(out.at[:, pl.ds(0, 6144)], out.at[:, pl.ds(0, 6144)], out_recv).wait()
+
+
+def fused(number, src, post, where, counts, over, queries, k_own, v_own, k_twin):
+    vmem = lambda *shape: pltpu.VMEM((*shape, BLK, HD), jnp.bfloat16)
+    smem, whole = pl.BlockSpec(memory_space=pltpu.SMEM), pl.BlockSpec(memory_space=pltpu.VMEM)
+    anywhere = pl.BlockSpec(memory_space=pl.ANY)
+    dma = pltpu.SemaphoreType.DMA
+    return pl.pallas_call(
+        fused_kernel,
+        out_shape=(jax.ShapeDtypeStruct((96, 8192), jnp.bfloat16), jax.ShapeDtypeStruct((1, 128), jnp.int32)),
+        in_specs=[smem, smem, smem, smem, whole, *[anywhere] * 4],
+        out_specs=(anywhere, whole),
+        scratch_shapes=[
+            vmem(256), vmem(256), vmem(2 * USUAL[0]), vmem(NZ * NW * 6),
+            *[vmem(2 * c) for c in USUAL] * 2,
+            vmem(NZ * NW * 6), vmem(NZ * NW * 6), vmem(5 * 64),
+            pltpu.VMEM((384, 16, HD), jnp.bfloat16),
+            pltpu.VMEM((384, 2048), jnp.bfloat16),
+            pltpu.VMEM((BLK * 16, HD), jnp.float32),
+            pltpu.VMEM((SEL * BLK, HD), jnp.bfloat16),
+            pltpu.VMEM((SEL * BLK, 2 * HD), jnp.bfloat16),
+            pltpu.VMEM((NW, 1, 128), jnp.int32),
+            pltpu.VMEM((4, 1, 128), jnp.int32),
+            dma, dma((2, 2)), dma, dma((2, 2, 10)), dma((2, 2, 10)), dma((2, NZ)), dma((2,)), dma((2, NZ)),
+            dma((NW + 4,)), dma((NW + 4,)), dma, dma, dma,
+        ],
+        compiler_params=pltpu.CompilerParams(
+            collective_id=number, has_side_effects=True, vmem_limit_bytes=60 * 2**20
+        ),
+        name="fused",
+    )(src, post, where, counts, over, queries, k_own, v_own, k_twin)
+
+
 def own_requests(blocks, counts):
     me = lax.axis_index("ctx")
     z = me // NW
@@ -490,15 +785,14 @@
     mine, where = own_requests(sel_blocks, sel_counts)
     counts = sel_counts.reshape(-1)
     table, src, post, over, k_twin = exchange_requests(mine, k_own)
-    k, v, over = exchange_tiles(1, USUAL, src, post, over, (k_own, v_own), (k_twin, None))
-    out, over = attend_all(2, where, counts, over, queries, k, v)
+    out, over = fused(1, src, post, where, counts, over, queries, k_own, v_own, k_twin)
 
     def again():
         src, post = full_plan(table)
         none = jnp.zeros((1, 128), jnp.int32)
-        k, _ = exchange_tiles(3, FULL, src, post, none, (k_own,), (None,))
-        v, _ = exchange_tiles(4, FULL, src, post, none, (v_own,), (None,))
-        return attend_all(5, where, counts, none, queries, k, v)[0]
+        k, _ = exchange_tiles(2, FULL, src, post, none, (k_own,), (None,))
+        v, _ = exchange_tiles(3, FULL, src, post, none, (v_own,), (None,))
+        return attend_all(4, where, counts, none, queries, k, v)[0]
 
     return lax.cond(over[0, 0] > 0, again, lambda: out)
 

time: 275 us -> 259 us (0.942)
  Pallas kernels: 267 us -> 250 us
    pallas_call x2 -> x1, Pallas kernels: 249 us -> 231 us  [fused(): pl.pallas_call(fused_kernel, out_shape=(jax.ShapeDtypeStruct((96, 8192),...]
where the time goes in v3:
time: 259 us; the launch traced here: 258 us
  Pallas kernels  250 us (97%)
  local copies, waits for them, and re-layouts  5.21 us (2%)
  other arithmetic  2.63 us (1%)
    pallas_call x1, Pallas kernels, fused(): pl.pallas_call(fused_kernel, out_shape=(jax.ShapeDtypeStruct((96, 8192),...  231 us
    pallas_call x1, Pallas kernels, exchange_requests(): pl.pallas_call(requests_kernel, out_shape=(ints(NZ, NW, 128), ints(8, 128...  18.4 us

profile of v3, /device:TPU:1, one launch (start us, length us, event | category | flops | bytes accessed | tf_op | source)
XLA Modules:
  0.0 258.4 jit_solution(169575682242005762)
XLA Ops:
  0.0 0.0 copy-start
  0.0 0.9 reshape.155
  0.9 0.8 copy.28
  1.7 0.1 lt.35.counts
  1.8 0.8 broadcast_compare_fusion
  2.5 0.1 reshape.165
  2.6 0.7 fusion.25
  3.3 1.0 convert_reduce_fusion
  4.4 0.1 select_reduce_fusion.1
  4.5 0.1 reshape.156
  4.6 0.6 pad.4.mine
  5.2 18.4 %requests.1 = (s32[8,8,128]{2,1,0:T(8,128)S(1)}, s32[8,128]{1,0:T(8,128)}, s32[8,128]{1,0:T(8,128)}, s32[1,128]{1,0:T(1,128)}, bf16[128,64,128]{2,1,0:T(8,128)(2,1)}) custom-call(s32[8,1,128]{2,1,0:T(1,128)} %pad.4.mine, s32[8,128]{1,0:T(8,128)} %constant.165.clone.kinds, f32[128,128]{1,0:T(8,128)} %constant.166.clone.within, ...), custom_call_target="tpu_custom_call" | custom-call | tf_op jit(solution)/shard_map/requests/pallas_call | solution.py:146
  23.6 0.0 copy-done
  23.6 231.4 %fused.1 = (bf16[96,8192]{1,0:T(8,128)(2,1)}, s32[1,128]{1,0:T(1,128)}) custom-call(s32[8,128]{1,0:T(8,128)} %get-tuple-element.40.src, s32[8,128]{1,0:T(8,128)} %get-tuple-element.41.post, s32[192]{0:T(256)S(1)} %get-tuple-element.85.where, s32[12]{0:T(128)S(1)} %lt.35.counts, s32[1,128]{1,0:T(1,128)} %get-tuple-element.42.over, ...), custom_call_target="tpu_custom_call" | custom-call | tf_op jit(solution)/shard_map/fused/pallas_call | solution.py:712
  255.6 0.2 conditional.1
  255.8 2.7 %copy.43 = bf16[96,8192]{1,0:T(8,128)(2,1)} copy(bf16[96,8192]{1,0:T(8,128)(2,1)} %get-tuple-element.47) | data formatting | bytes 3145728
  (2 shorter events, 0.0 us)
Async XLA Ops:
  0.0 23.6 %copy-start = (bf16[2,4096,128]{2,1,0:T(8,128)(2,1)S(1)}, bf16[2,4096,128]{2,1,0:T(8,128)(2,1)}, u32[]{:S(2)}) copy-start(bf16[2,4096,128]{2,1,0:T(8,128)(2,1)} %param.17) | copy-start | bytes 6291460

commit v4 on v3

--- a/solution.py
+++ b/solution.py
@@ -20,146 +20,6 @@
 
 def at_ctx(index):
     return {"ctx": index}
-
-
-def requests_kernel(
-    mine, kinds, within, same, lower, column, k_own,
-    table, src, post, over, k_twin,
-    rows, local_sem, send_sem, recv_sem,
-):
-    me = lax.axis_index("ctx")
-    z, w = me // NW, me % NW
-    barrier = pltpu.get_barrier_semaphore()
-    for r in range(1, 8):
-        pl.semaphore_signal(barrier, inc=1, device_id=at_ctx(z * NW + (w + r) % NW), device_id_type=MESH)
-        pl.semaphore_signal(barrier, inc=1, device_id=at_ctx((z + r) % NZ * NW + w), device_id_type=MESH)
-    pl.semaphore_wait(barrier, 14)
-
-    own = pltpu.make_async_copy(mine.at[pl.ds(w, 1)], rows.at[pl.ds(w, 1)], local_sem)
-    own.start()
-    inside = []
-    for r in range(1, NW):
-        ow = (w + r) % NW
-        copy = pltpu.make_async_remote_copy(
-            src_ref=mine.at[pl.ds(ow, 1)], dst_ref=rows.at[pl.ds(w, 1)],
-            send_sem=send_sem.at[r], recv_sem=recv_sem.at[r],
-            device_id=at_ctx(z * NW + ow), device_id_type=MESH,
-        )
-        copy.start()
-        inside.append(copy)
-    keys_over = pltpu.make_async_remote_copy(
-        src_ref=k_own, dst_ref=k_twin, send_sem=send_sem.at[0], recv_sem=recv_sem.at[0],
-        device_id=at_ctx(me + 1 - 2 * (me % 2)), device_id_type=MESH,
-    )
-    keys_over.start()
-    own.wait()
-    for copy in inside:
-        copy.wait()
-    table[0] = jnp.concatenate([rows[i] for i in range(NW)], axis=0)
-    along = []
-    for r in range(1, NZ):
-        copy = pltpu.make_async_remote_copy(
-            src_ref=table.at[0], dst_ref=table.at[NZ - r],
-            send_sem=send_sem.at[NW + r], recv_sem=recv_sem.at[NW + r],
-            device_id=at_ctx((z + r) % NZ * NW + w), device_id_type=MESH,
-        )
-        copy.start()
-        along.append(copy)
-    for copy in along:
-        copy.wait()
-
-    kind = kinds[...]
-    asked = [table[i] for i in range(NZ)]
-    by_source = []
-    for i in range(NZ):
-        row = jnp.zeros((NW, 128), jnp.int32)
-        for k in range(NZ):
-            row = jnp.where(kind == k, asked[(i + k) % NZ], row)
-        by_source.append(row)
-    tiles = jnp.concatenate(by_source, axis=0)
-    kind = jnp.concatenate([kind] * NZ, axis=0)
-    live = tiles > 0
-    ones = live.astype(jnp.float32)
-    dot = lambda x, y: jnp.dot(x, y, preferred_element_type=jnp.float32)
-    per_row = dot(ones, same[...])
-    at = dot(ones, within[...]) + dot(lower[...], per_row)
-    sums = dot(column[...], per_row)
-    n = [sums[:, 6 * k:6 * k + 1] for k in range(NZ)]
-    c1, c2, c3, c4 = (float(c) for c in USUAL)
-    least = lambda x, y, t: jnp.minimum(
-        jnp.minimum(jnp.full_like(x, c4), c3 - x), jnp.minimum(c2 - x - y, c1 - x - y - t)
-    )
-    room_up, room_down = least(n[3], n[2], n[1]), least(n[5], n[6], n[7])
-    four_up = jnp.clip(room_up, 0.0, n[4])
-    four_down = n[4] - four_up
-    short = (room_up < 0) | (room_down < 0) | (four_down > room_down)
-    over[...] = jnp.broadcast_to(jnp.max(short.astype(jnp.float32), axis=0, keepdims=True), (1, 128)).astype(jnp.int32)
-    up = (kind < 4) | ((kind == 4) & (at < four_up))
-    base = jnp.zeros_like(at)
-    for k, first in (
-        (3, four_up), (2, four_up + n[3]), (1, four_up + n[3] + n[2]),
-        (5, four_down), (6, four_down + n[5]), (7, four_down + n[5] + n[6]),
-    ):
-        base = jnp.where(kind == k, first, base)
-    base = jnp.where((kind == 4) & (at >= four_up), -four_up, base)
-    at = at + base
-
-    places = lax.broadcasted_iota(jnp.int32, (128, 128), 0).astype(jnp.float32)
-    found = []
-    for way in range(2):
-        mine_too = live[0:NW] & (up[0:NW] if way == 0 else ~up[0:NW]) & (kind[0:NW] > 0)
-        place = jnp.where(mine_too, at[0:NW], -1.0)
-        value = jnp.where(mine_too, tiles[0:NW], 0).astype(jnp.float32)
-        total = jnp.zeros((128, 128), jnp.float32)
-        for i in range(NW):
-            total = jnp.where(place[i:i + 1] == places, value[i:i + 1], total)
-        found.append(
-            lax.dot_general(
-                jnp.ones((8, 128), jnp.float32), total, (((1,), (1,)), ((), ())), preferred_element_type=jnp.float32
-            )
-        )
-    row = lax.broadcasted_iota(jnp.int32, (8, 128), 0)
-    src[...] = jnp.maximum(jnp.where(row == 0, found[0], found[1]).astype(jnp.int32) - 1, 0)
-
-    cap = jnp.full((NZ * NW, 128), c1)
-    for k in range(2, 7):
-        cap = jnp.where(kind == k, (c1, c2, c3, c4)[min(k, NZ - k) - 1], cap)
-    spot = jnp.clip(at, 0.0, cap - 1) + jnp.where(up, 0.0, cap)
-    spot = spot.astype(jnp.int32)
-    mine_at = jnp.maximum(tiles[0:NW] - 1, 0)
-    for k in range(1, NZ):
-        i = NZ - k
-        mine_at = jnp.where(kind[0:NW] == k, spot[i * NW:(i + 1) * NW], mine_at)
-    post[...] = mine_at
-    keys_over.wait()
-
-
-def exchange_requests(mine, k_own):
-    vmem, anywhere = pl.BlockSpec(memory_space=pltpu.VMEM), pl.BlockSpec(memory_space=pl.ANY)
-    lane, row = np.arange(128), np.arange(NZ * NW)
-    block = (lane[:, None] // 6 == lane[None, :] // 6) & (lane[:, None] < 48)
-    plane = row[:, None] // NW == row[None, :] // NW
-    kinds = np.broadcast_to(np.where(lane < 48, lane // 6, 9), (NW, 128)).astype(np.int32)
-    within = (block & (lane[:, None] < lane[None, :])).astype(np.float32)
-    lower = (plane & (row[None, :] < row[:, None])).astype(np.float32)
-    ints = lambda *shape: jax.ShapeDtypeStruct(shape, jnp.int32)
-    return pl.pallas_call(
-        requests_kernel,
-        out_shape=(
-            ints(NZ, NW, 128), ints(8, 128), ints(NW, 128), ints(1, 128),
-            jax.ShapeDtypeStruct(k_own.shape, k_own.dtype),
-        ),
-        in_specs=[*[vmem] * 6, anywhere],
-        out_specs=(*[vmem] * 4, anywhere),
-        scratch_shapes=[
-            pltpu.VMEM((NW, 1, 128), jnp.int32),
-            pltpu.SemaphoreType.DMA,
-            pltpu.SemaphoreType.DMA((16,)),
-            pltpu.SemaphoreType.DMA((16,)),
-        ],
-        compiler_params=pltpu.CompilerParams(collective_id=0, has_side_effects=True),
-        name="requests",
-    )(mine, kinds, within, block.astype(np.float32), lower, plane.astype(np.float32), k_own)
 
 
 def tiles_kernel(caps, arrays, fetch, src, post, over, *refs):
@@ -441,11 +301,11 @@
 
 
 def fused_kernel(
-    src, post, where, counts, over, q_in, k_own, v_own, k_twin, out, over_out,
+    asks, within, same, lower, column, counts, q_in, k_own, v_own, out, over_out, table, where_v,
     tab_k, tab_v, packed, stage, k1, k2, k3, k4, v1, v2, v3, v4, land_k, land_v, more,
-    q, merged, qf, kc, vc, overs, overs_head,
+    q, merged, qf, kc, vc, overs, overs_head, mine, rows, src_v, post_v, src, post, where,
     q_sem, tab_sem, twin_send, z_send, z_recv, y_send, y_recv, y_local,
-    over_send, over_recv, out_send, out_recv, out_own,
+    over_send, over_recv, out_send, out_recv, out_own, local_sem, ask_send, ask_recv, plan_sem,
 ):
     caps = USUAL
     cuts = (0, *caps[::-1])
@@ -457,35 +317,160 @@
     towards = (((z + 1) % NZ) * NW + w, ((z + NZ - 1) % NZ) * NW + w)
 
     barrier = pltpu.get_barrier_semaphore()
-    for other in towards:
-        pl.semaphore_signal(barrier, inc=1, device_id=at_ctx(other), device_id_type=MESH)
-    for r in range(1, NW):
+    for r in range(1, 8):
         pl.semaphore_signal(barrier, inc=1, device_id=at_ctx(z * NW + (w + r) % NW), device_id_type=MESH)
+        pl.semaphore_signal(barrier, inc=1, device_id=at_ctx((z + r) % NZ * NW + w), device_id_type=MESH)
     for r in range(1, 4):
         pl.semaphore_signal(barrier, inc=1, device_id={"head": (head + r) % 4}, device_id_type=MESH)
-    pl.semaphore_wait(barrier, NW + 4)
+
+    size = asks.shape[1]
+    ask = asks[...]
+    across = jnp.broadcast_to(ask.astype(jnp.float32), (size, size))
+    down = across.T.astype(jnp.int32)
+    i0 = lax.broadcasted_iota(jnp.int32, (size, size), 0)
+    i1 = lax.broadcasted_iota(jnp.int32, (size, size), 1)
+    earlier = ((down >> 6) == (jnp.broadcast_to(ask, (size, size)) >> 6)) & (i0 < i1)
+    rank = jnp.sum(earlier.astype(jnp.float32), axis=0, keepdims=True).astype(jnp.int32)
+    used = ask >= 0
+    holder = ask >> 6
+    its_core = holder & 1
+    lane = ((holder >> 1) & 3) * 2 + ((rank + its_core) & 1)
+    away = (z - (holder >> 3) + NZ) & 7
+    inside = its_core * 3 + (rank >> 1)
+    group = (lax.broadcasted_iota(jnp.int32, (1, size), 1) >> 4) & 1
+    tile = its_core * 128 + group * BLK + (ask & 63) + 1
+    where_v[...] = jnp.clip(jnp.where(used, away * 48 + lane * 6 + inside, 0), 0, NZ * NW * 6 - 1)
+    to_lane = lax.broadcasted_iota(jnp.int32, (NW, size), 0) == jnp.where(used, lane, -1)
+    to_slot = lax.broadcasted_iota(jnp.int32, (128, size), 0) == away * 6 + inside
+    asked_of = lax.dot_general(
+        jnp.where(to_lane, tile.astype(jnp.float32), 0.0), to_slot.astype(jnp.float32),
+        (((1,), (1,)), ((), ())), preferred_element_type=jnp.float32,
+    ).astype(jnp.int32)
+    for i in range(NW):
+        mine[i] = asked_of[i:i + 1]
+
+    pl.semaphore_wait(barrier, 17)
+
+    asking = []
+    for r in range(1, NW):
+        ow = (w + r) % NW
+        copy = pltpu.make_async_remote_copy(
+            src_ref=mine.at[pl.ds(ow, 1)], dst_ref=rows.at[pl.ds(w, 1)],
+            send_sem=ask_send.at[r], recv_sem=ask_recv.at[r],
+            device_id=at_ctx(z * NW + ow), device_id_type=MESH,
+        )
+        copy.start()
+        asking.append(copy)
+    own = pltpu.make_async_copy(mine.at[pl.ds(w, 1)], rows.at[pl.ds(w, 1)], local_sem)
+    own.start()
 
     mine_k, mine_v = (t.at[pl.ds(core * 128, 128)] for t in tab)
-    twin_k = tab_k.at[pl.ds((1 - core) * 128, 128)]
-    loads = (
-        (pltpu.make_async_copy(k_own, mine_k, tab_sem.at[0, 0]), pltpu.make_async_copy(k_twin, twin_k, tab_sem.at[0, 1])),
-        (
-            pltpu.make_async_copy(v_own, mine_v, tab_sem.at[1, 0]),
+    loads = []
+    for a, (ref, near) in enumerate(((k_own, mine_k), (v_own, mine_v))):
+        pair = (
+            pltpu.make_async_copy(ref, near, tab_sem.at[a, 0]),
             pltpu.make_async_remote_copy(
-                src_ref=v_own, dst_ref=mine_v, send_sem=twin_send, recv_sem=tab_sem.at[1, 1],
+                src_ref=ref, dst_ref=near, send_sem=twin_send.at[a], recv_sem=tab_sem.at[a, 1],
                 device_id=at_ctx(me + 1 - 2 * core), device_id_type=MESH,
             ),
-        ),
-    )
-    for pair in loads:
+        )
         for copy in pair:
             copy.start()
+        loads.append(pair)
     q_load = pltpu.make_async_copy(q_in, q, q_sem)
     q_load.start()
+
+    own.wait()
+    for copy in asking:
+        copy.wait()
+    table[0] = jnp.concatenate([rows[i] for i in range(NW)], axis=0)
+    asking = []
+    for r in range(1, NZ):
+        copy = pltpu.make_async_remote_copy(
+            src_ref=table.at[0], dst_ref=table.at[NZ - r],
+            send_sem=ask_send.at[NW + r], recv_sem=ask_recv.at[NW + r],
+            device_id=at_ctx((z + r) % NZ * NW + w), device_id_type=MESH,
+        )
+        copy.start()
+        asking.append(copy)
+    for copy in asking:
+        copy.wait()
+
+    kind = (lax.broadcasted_iota(jnp.int32, (NW, 128), 1) * 43) >> 8
+    asked = [table[i] for i in range(NZ)]
+    by_source = []
+    for i in range(NZ):
+        row = jnp.zeros((NW, 128), jnp.int32)
+        for k in range(NZ):
+            row = jnp.where(kind == k, asked[(i + k) % NZ], row)
+        by_source.append(row)
+    tiles = jnp.concatenate(by_source, axis=0)
+    kind = jnp.concatenate([kind] * NZ, axis=0)
+    live = tiles > 0
+    ones = live.astype(jnp.float32)
+    dot = lambda x, y: jnp.dot(x, y, preferred_element_type=jnp.float32)
+    per_row = dot(ones, same[...])
+    at = dot(ones, within[...]) + dot(lower[...], per_row)
+    sums = dot(column[...], per_row)
+    n = [sums[:, 6 * k:6 * k + 1] for k in range(NZ)]
+    c1, c2, c3, c4 = (float(c) for c in USUAL)
+    least = lambda x, y, t: jnp.minimum(
+        jnp.minimum(jnp.full_like(x, c4), c3 - x), jnp.minimum(c2 - x - y, c1 - x - y - t)
+    )
+    room_up, room_down = least(n[3], n[2], n[1]), least(n[5], n[6], n[7])
+    four_up = jnp.clip(room_up, 0.0, n[4])
+    four_down = n[4] - four_up
+    short = (room_up < 0) | (room_down < 0) | (four_down > room_down)
+    over = jnp.broadcast_to(jnp.max(short.astype(jnp.float32), axis=0, keepdims=True), (1, 128)).astype(jnp.int32)
+    up = (kind < 4) | ((kind == 4) & (at < four_up))
+    base = jnp.zeros_like(at)
+    for k, first in (
+        (3, four_up), (2, four_up + n[3]), (1, four_up + n[3] + n[2]),
+        (5, four_down), (6, four_down + n[5]), (7, four_down + n[5] + n[6]),
+    ):
+        base = jnp.where(kind == k, first, base)
+    base = jnp.where((kind == 4) & (at >= four_up), -four_up, base)
+    at = at + base
+
+    places = lax.broadcasted_iota(jnp.int32, (128, 128), 0).astype(jnp.float32)
+    found = []
+    for way in range(2):
+        mine_too = live[0:NW] & (up[0:NW] if way == 0 else ~up[0:NW]) & (kind[0:NW] > 0)
+        place = jnp.where(mine_too, at[0:NW], -1.0)
+        value = jnp.where(mine_too, tiles[0:NW], 0).astype(jnp.float32)
+        total = jnp.zeros((128, 128), jnp.float32)
+        for i in range(NW):
+            total = jnp.where(place[i:i + 1] == places, value[i:i + 1], total)
+        found.append(
+            lax.dot_general(
+                jnp.ones((8, 128), jnp.float32), total, (((1,), (1,)), ((), ())), preferred_element_type=jnp.float32
+            )
+        )
+    row = lax.broadcasted_iota(jnp.int32, (8, 128), 0)
+    src_v[...] = jnp.clip(jnp.where(row == 0, found[0], found[1]).astype(jnp.int32) - 1, 0, 255)
+
+    cap = jnp.full((NZ * NW, 128), USUAL[0], jnp.int32)
+    for k in range(2, 7):
+        cap = jnp.where(kind == k, USUAL[min(k, NZ - k) - 1], cap)
+    spot = jnp.clip(at.astype(jnp.int32), 0, cap - 1) + jnp.where(up, 0, cap)
+    mine_at = jnp.clip(tiles[0:NW] - 1, 0, 255)
+    for k in range(1, NZ):
+        i = NZ - k
+        mine_at = jnp.where(kind[0:NW] == k, spot[i * NW:(i + 1) * NW], mine_at)
+    post_v[...] = mine_at
+    moves = [
+        pltpu.make_async_copy(ref, to, plan_sem.at[i])
+        for i, (ref, to) in enumerate(((src_v, src), (post_v, post), (where_v, where)))
+    ]
+    for copy in moves:
+        copy.start()
+    for copy in moves:
+        copy.wait()
+    overs[0] = over
     told = []
     for r in range(1, NW):
         copy = pltpu.make_async_remote_copy(
-            src_ref=over, dst_ref=overs.at[r], send_sem=over_send.at[r], recv_sem=over_recv.at[r],
+            src_ref=overs.at[0], dst_ref=overs.at[r], send_sem=over_send.at[r], recv_sem=over_recv.at[r],
             device_id=at_ctx(z * NW + (w + r) % NW), device_id_type=MESH,
         )
         copy.start()
@@ -569,7 +554,7 @@
         qf[...] = q[pl.ds(b * BLK, BLK)].astype(jnp.float32).reshape(BLK * 16, HD)
 
         def gather(i, c):
-            kc[pl.ds(i * BLK, BLK)] = land_k[where[item * SEL + i]]
+            kc[pl.ds(i * BLK, BLK)] = land_k[where[0, item * SEL + i]]
             return c
 
         lax.fori_loop(0, SEL, gather, 0)
@@ -590,7 +575,7 @@
         b, g = item // 2, item % 2
 
         def gather(i, c):
-            vc[pl.ds(i * BLK, BLK), 0:HD] = land_v[where[item * SEL + i]]
+            vc[pl.ds(i * BLK, BLK), 0:HD] = land_v[where[0, item * SEL + i]]
             return c
 
         lax.fori_loop(0, SEL, gather, 0)
@@ -665,7 +650,7 @@
     deliver(1, 5)
     vc[:, HD:] = jnp.ones((keys, HD), jnp.bfloat16)
     q_load.wait()
-    most = over[...]
+    most = over
     for r, copy in enumerate(told):
         copy.wait()
         most = jnp.maximum(most, overs[r + 1])
@@ -704,16 +689,27 @@
     pltpu.make_async_copy(out.at[:, pl.ds(0, 6144)], out.at[:, pl.ds(0, 6144)], out_recv).wait()
 
 
-def fused(number, src, post, where, counts, over, queries, k_own, v_own, k_twin):
+def fused(number, asks, counts, queries, k_own, v_own):
     vmem = lambda *shape: pltpu.VMEM((*shape, BLK, HD), jnp.bfloat16)
+    ints = lambda *shape: pltpu.VMEM(shape, jnp.int32)
     smem, whole = pl.BlockSpec(memory_space=pltpu.SMEM), pl.BlockSpec(memory_space=pltpu.VMEM)
     anywhere = pl.BlockSpec(memory_space=pl.ANY)
     dma = pltpu.SemaphoreType.DMA
+    lane, row = np.arange(128), np.arange(NZ * NW)
+    block = (lane[:, None] // 6 == lane[None, :] // 6) & (lane[:, None] < 48)
+    plane = row[:, None] // NW == row[None, :] // NW
+    within = (block & (lane[:, None] < lane[None, :])).astype(np.float32)
+    lower = (plane & (row[None, :] < row[:, None])).astype(np.float32)
     return pl.pallas_call(
         fused_kernel,
-        out_shape=(jax.ShapeDtypeStruct((96, 8192), jnp.bfloat16), jax.ShapeDtypeStruct((1, 128), jnp.int32)),
-        in_specs=[smem, smem, smem, smem, whole, *[anywhere] * 4],
-        out_specs=(anywhere, whole),
+        out_shape=(
+            jax.ShapeDtypeStruct((96, 8192), jnp.bfloat16),
+            jax.ShapeDtypeStruct((1, 128), jnp.int32),
+            jax.ShapeDtypeStruct((NZ, NW, 128), jnp.int32),
+            jax.ShapeDtypeStruct(asks.shape, jnp.int32),
+        ),
+        in_specs=[*[whole] * 5, smem, *[anywhere] * 3],
+        out_specs=(anywhere, whole, whole, whole),
         scratch_shapes=[
             vmem(256), vmem(256), vmem(2 * USUAL[0]), vmem(NZ * NW * 6),
             *[vmem(2 * c) for c in USUAL] * 2,
@@ -723,37 +719,16 @@
             pltpu.VMEM((BLK * 16, HD), jnp.float32),
             pltpu.VMEM((SEL * BLK, HD), jnp.bfloat16),
             pltpu.VMEM((SEL * BLK, 2 * HD), jnp.bfloat16),
-            pltpu.VMEM((NW, 1, 128), jnp.int32),
-            pltpu.VMEM((4, 1, 128), jnp.int32),
-            dma, dma((2, 2)), dma, dma((2, 2, 10)), dma((2, 2, 10)), dma((2, NZ)), dma((2,)), dma((2, NZ)),
-            dma((NW + 4,)), dma((NW + 4,)), dma, dma, dma,
+            ints(NW, 1, 128), ints(4, 1, 128), ints(NW, 1, 128), ints(NW, 1, 128), ints(8, 128), ints(8, 128),
+            pltpu.SMEM((8, 128), jnp.int32), pltpu.SMEM((8, 128), jnp.int32), pltpu.SMEM(asks.shape, jnp.int32),
+            dma, dma((2, 2)), dma((2,)), dma((2, 2, 10)), dma((2, 2, 10)), dma((2, NZ)), dma((2,)), dma((2, NZ)),
+            dma((NW + 4,)), dma((NW + 4,)), dma, dma, dma, dma, dma((16,)), dma((16,)), dma((3,)),
         ],
         compiler_params=pltpu.CompilerParams(
             collective_id=number, has_side_effects=True, vmem_limit_bytes=60 * 2**20
         ),
         name="fused",
-    )(src, post, where, counts, over, queries, k_own, v_own, k_twin)
-
-
-def own_requests(blocks, counts):
-    me = lax.axis_index("ctx")
-    z = me // NW
-    flat = blocks.reshape(-1)
-    ids = np.arange(ITEMS * SEL)
-    live = (jnp.asarray(ids % SEL)[None, :].reshape(ITEMS, SEL) < counts.reshape(ITEMS, 1)).reshape(-1)
-    holder = jnp.where(live, flat // BLK, -1)
-    earlier = jnp.asarray(ids[None, :] < ids[:, None])
-    rank = jnp.sum(((holder[:, None] == holder[None, :]) & earlier).astype(jnp.int32), axis=1)
-    core = holder % 2
-    lane = (holder // 2 % 4) * 2 + (rank + core) % 2
-    away = (z - holder // NW + NZ) % NZ
-    inside = core * 3 + rank // 2
-    tile = core * 128 + jnp.asarray(ids // SEL % 2) * BLK + flat % BLK + 1
-    slot = jnp.where(live, lane * 48 + away * 6 + inside, -1)
-    mine = jnp.sum(jnp.where(slot[None, :] == jnp.arange(NW * 48)[:, None], tile[None, :], 0), axis=1)
-    mine = jnp.pad(mine.reshape(NW, 1, 48), ((0, 0), (0, 0), (0, 80)))
-    where = jnp.where(live, away * 48 + lane * 6 + inside, 0)
-    return mine, where
+    )(asks, within, block.astype(np.float32), lower, plane.astype(np.float32), counts, queries, k_own, v_own)
 
 
 def full_plan(table):
@@ -782,17 +757,18 @@
 def per_device(queries, keys, values, sel_blocks, sel_counts):
     k_own = keys.reshape(128, BLK, HD)
     v_own = values.reshape(128, BLK, HD)
-    mine, where = own_requests(sel_blocks, sel_counts)
     counts = sel_counts.reshape(-1)
-    table, src, post, over, k_twin = exchange_requests(mine, k_own)
-    out, over = fused(1, src, post, where, counts, over, queries, k_own, v_own, k_twin)
+    used = np.arange(SEL)[None, None, :] < sel_counts[:, :, None]
+    asks = jnp.where(used, sel_blocks, -1).reshape(1, ITEMS * SEL)
+    asks = jnp.pad(asks, ((0, 0), (0, 256 - ITEMS * SEL)), constant_values=-1)
+    out, over, table, where = fused(1, asks, counts, queries, k_own, v_own)
 
     def again():
         src, post = full_plan(table)
         none = jnp.zeros((1, 128), jnp.int32)
         k, _ = exchange_tiles(2, FULL, src, post, none, (k_own,), (None,))
         v, _ = exchange_tiles(3, FULL, src, post, none, (v_own,), (None,))
-        return attend_all(4, where, counts, none, queries, k, v)[0]
+        return attend_all(4, where[0, :ITEMS * SEL], counts, none, queries, k, v)[0]
 
     return lax.cond(over[0, 0] > 0, again, lambda: out)
 

time: 259 us -> 249 us (0.961)
  Pallas kernels: 250 us -> 243 us
    pallas_call x1 -> x0, Pallas kernels: 18.4 us -> none  [exchange_requests(): pl.pallas_call(requests_kernel, out_shape=(ints(NZ, NW, 128), ints(8, 128...]
    pallas_call x1, Pallas kernels: 231 us -> 243 us  [fused(): pl.pallas_call(fused_kernel, out_shape=(jax.ShapeDtypeStruct((96, 8192),...]
where the time goes in v4:
time: 249 us
  Pallas kernels  243 us (98%)
  local copies, waits for them, and re-layouts  4.16 us (2%)
    pallas_call x1, Pallas kernels, fused(): pl.pallas_call(fused_kernel, out_shape=(jax.ShapeDtypeStruct((96, 8192),...  243 us

profile of v4, /device:TPU:1, one launch (start us, length us, event | category | flops | bytes accessed | tf_op | source)
XLA Modules:
  0.0 248.9 jit_solution(3571035508431830259)
XLA Ops:
  0.0 0.8 copy.27
  0.8 0.1 reshape.148.counts
  0.8 0.8 compare_select_fusion
  1.6 0.1 reshape.147
  1.7 0.6 pad.4.asks
  2.3 0.0 copy-start
  2.3 243.0 %fused.1 = (bf16[96,8192]{1,0:T(8,128)(2,1)}, s32[1,128]{1,0:T(1,128)}, s32[8,8,128]{2,1,0:T(8,128)S(1)}, s32[1,256]{1,0:T(1,128)S(1)}) custom-call(s32[1,256]{1,0:T(1,128)} %pad.4.asks, f32[128,128]{1,0:T(8,128)} %constant.17.clone.within, f32[128,128]{1,0:T(8,128)} %constant.46.clone.same, f32[64,64]{1,0:T(8,128)} %constant.47.clone.lower, ...), custom_call_target="tpu_custom_call" | custom-call | tf_op jit(solution)/shard_map/fused/pallas_call | solution.py:703
  246.0 0.0 copy-done
  246.0 0.2 conditional.1
  246.2 2.7 %copy.42 = bf16[96,8192]{1,0:T(8,128)(2,1)} copy(bf16[96,8192]{1,0:T(8,128)(2,1)} %get-tuple-element.41) | data formatting | bytes 3145728
Async XLA Ops:
  2.3 243.7 %copy-start = (bf16[2,4096,128]{2,1,0:T(8,128)(2,1)S(1)}, bf16[2,4096,128]{2,1,0:T(8,128)(2,1)}, u32[]{:S(2)}) copy-start(bf16[2,4096,128]{2,1,0:T(8,128)(2,1)} %param.14) | copy-start | bytes 6291460

commit v5 on v4

--- a/solution.py
+++ b/solution.py
@@ -548,8 +548,12 @@
     factor = float(HD ** -0.5 * np.log2(np.e))
     first = ((head + 1) * 3 // 2) % 6 * 2
 
+    def item_of(n):
+        i = n // 2
+        return (first + (i * 3 + i // 2) % 6 * 2 + n % 2) % ITEMS
+
     def weigh(ref, n, spot):
-        item = (first + n) % ITEMS
+        item = item_of(n)
         b, g = item // 2, item % 2
         qf[...] = q[pl.ds(b * BLK, BLK)].astype(jnp.float32).reshape(BLK * 16, HD)
 
@@ -571,7 +575,7 @@
                 ref[spot * 64 + h * 8 + c] = p[h * BLK:(h + 1) * BLK, c * HD:(c + 1) * HD]
 
     def finish(ref, n, spot):
-        item = (first + n) % ITEMS
+        item = item_of(n)
         b, g = item // 2, item % 2
 
         def gather(i, c):

time: 249 us -> 249 us (level)
  no operation moved by 1% of the time
where the time goes in v5:
time: 249 us
  Pallas kernels  243 us (98%)
  local copies, waits for them, and re-layouts  4.16 us (2%)
    pallas_call x1, Pallas kernels, fused(): pl.pallas_call(fused_kernel, out_shape=(jax.ShapeDtypeStruct((96, 8192),...  243 us

profile of v5, /device:TPU:1, one launch (start us, length us, event | category | flops | bytes accessed | tf_op | source)
XLA Modules:
  0.0 248.9 jit_solution(6974310742089036100)
XLA Ops:
  0.0 0.8 copy.27
  0.8 0.1 reshape.148.counts
  0.8 0.8 compare_select_fusion
  1.6 0.1 reshape.147
  1.7 0.6 pad.4.asks
  2.3 0.0 copy-start
  2.3 243.1 %fused.1 = (bf16[96,8192]{1,0:T(8,128)(2,1)}, s32[1,128]{1,0:T(1,128)}, s32[8,8,128]{2,1,0:T(8,128)S(1)}, s32[1,256]{1,0:T(1,128)S(1)}) custom-call(s32[1,256]{1,0:T(1,128)} %pad.4.asks, f32[128,128]{1,0:T(8,128)} %constant.17.clone.within, f32[128,128]{1,0:T(8,128)} %constant.46.clone.same, f32[64,64]{1,0:T(8,128)} %constant.47.clone.lower, ...), custom_call_target="tpu_custom_call" | custom-call | tf_op jit(solution)/shard_map/fused/pallas_call | solution.py:707
  246.1 0.0 copy-done
  246.1 0.2 conditional.1
  246.3 2.7 %copy.42 = bf16[96,8192]{1,0:T(8,128)(2,1)} copy(bf16[96,8192]{1,0:T(8,128)(2,1)} %get-tuple-element.41) | data formatting | bytes 3145728
Async XLA Ops:
  2.3 243.8 %copy-start = (bf16[2,4096,128]{2,1,0:T(8,128)(2,1)S(1)}, bf16[2,4096,128]{2,1,0:T(8,128)(2,1)}, u32[]{:S(2)}) copy-start(bf16[2,4096,128]{2,1,0:T(8,128)(2,1)} %param.14) | copy-start | bytes 6291460
